TPU v7x, 256 devices: a whole 4x4x8 slice. The times are simulated.
256 devices in a mesh: section: 16 (over z, core), expert: 16 (over y, x).
Axes of the slice: x: 4, y: 4, z: 8, core: 2. Of those that a mesh axis runs over, the one named last changes fastest.
Arguments:
- section_layer_input: bfloat16 [16, 2048, 4096], P('section', 'expert'), may hold values from -6 to 6
- token_expert_choice: int32 [16, 2048, 8], P('section', 'expert'), may hold values from 0 to 127, as said below
- route_gate_steps: int32 [16, 2048, 8], P('section', 'expert'), may hold values from 1 to 4096
- gate_weight: bfloat16 [16, 4096, 4096], P('section', 'expert'), may hold values from -0.09375 to 0.09375
- up_weight: bfloat16 [16, 4096, 4096], P('section', 'expert'), may hold values from -0.09375 to 0.09375
- down_weight: bfloat16 [16, 4096, 4096], P('section', 'expert'), may hold values from -0.1875 to 0.1875
- adapter_down_maps: bfloat16 [16, 4096, 16], P('section', 'expert'), may hold values from -0.1875 to 0.1875
- adapter_up_maps: bfloat16 [16, 4, 16, 4096], P('section'), may hold values from -1.5 to 1.5
- cotangent: bfloat16 [16, 2048, 4096], P('section', 'expert'), may hold values from -6 to 6
Outputs:
- next_input: bfloat16 [16, 2048, 4096], P('section', 'expert')
- prev_grad: bfloat16 [16, 2048, 4096], P('section', 'expert')
- adapter_a_grad: float32 [16, 4096, 16], P('section', 'expert')
- adapter_b_grad: float32 [16, 4, 16, 4096], P('section', None, None, 'expert')
Inputs may be any that keep to these rules, and one draw needn't show every extreme that they name: `token_expert_choice`: every token names 8 different experts. The experts below 4 are those in flight; the tokens of one device (aligned blocks of 128 tokens of a section) name any one of them at most 16 times, and in every section one of them is named exactly 16 times by the tokens of every device.
All inputs are finite; a program needn't handle non-finite values.
Results may differ from a plain program's by a relative error of at most 0.0069.
Values may be sent and summed in bfloat16 or wider, within the bound.
A program may use at most 64 MiB of HBM per device.

v0:
```python
import jax
import jax.numpy as jnp
from jax import lax
from jax.sharding import PartitionSpec as P

SPLIT = 4
MOST = 16


LOWRANK_SCALE = 2.0
LEVEL_STEP = 1.0 / 4096.0


def from_behind(block, axis, distance):
    devices = range(lax.axis_size(axis))
    route = [((i - distance) % len(devices), i) for i in devices]
    return lax.ppermute(block, axis, route)


def expert_forward(in_rows, gate_proj, up_proj, down_proj, down_adapter_factor, up_adapter_factor):
    contract_last = (((1,), (1,)), ((), ()))
    pre_gate = lax.dot_general(
        in_rows, gate_proj, contract_last, preferred_element_type=jnp.float32
    )
    pre_up = lax.dot_general(in_rows, up_proj, contract_last, preferred_element_type=jnp.float32)
    hidden = (jax.nn.silu(pre_gate) * pre_up).astype(jnp.bfloat16)
    projected_hidden = jnp.dot(
        hidden, down_adapter_factor, preferred_element_type=jnp.float32
    ).astype(jnp.bfloat16)
    layer_result_rows = jnp.dot(hidden, down_proj, preferred_element_type=jnp.float32)
    layer_result_rows = (
        layer_result_rows
        + LOWRANK_SCALE
        * jnp.dot(projected_hidden, up_adapter_factor, preferred_element_type=jnp.float32)
    ).astype(jnp.bfloat16)
    return (pre_gate, pre_up, hidden, projected_hidden, layer_result_rows)


def expert_backward(
    grad_in_rows,
    pre_gate,
    pre_up,
    gate_proj,
    up_proj,
    down_proj,
    down_adapter_factor,
    up_adapter_factor,
):
    contract_last = (((1,), (1,)), ((), ()))
    adapter_product = lax.dot_general(
        grad_in_rows, up_adapter_factor, contract_last, preferred_element_type=jnp.float32
    )
    adapter_product = (LOWRANK_SCALE * adapter_product).astype(jnp.bfloat16)
    grad_hidden = lax.dot_general(
        grad_in_rows, down_proj, contract_last, preferred_element_type=jnp.float32
    )
    grad_hidden = grad_hidden + lax.dot_general(
        adapter_product, down_adapter_factor, contract_last, preferred_element_type=jnp.float32
    )
    sigmoid_gate = jax.nn.sigmoid(pre_gate)
    grad_gate = (
        grad_hidden * pre_up * sigmoid_gate * (1.0 + pre_gate * (1.0 - sigmoid_gate))
    ).astype(jnp.bfloat16)
    grad_up = (grad_hidden * pre_gate * sigmoid_gate).astype(jnp.bfloat16)
    grad_input = jnp.dot(grad_gate, gate_proj, preferred_element_type=jnp.float32)
    grad_input = (
        grad_input + jnp.dot(grad_up, up_proj, preferred_element_type=jnp.float32)
    ).astype(jnp.bfloat16)
    return (adapter_product, grad_input)


def on_device(
    section_layer_input,
    token_expert_choice,
    route_gate_steps,
    gate_weight,
    up_weight,
    down_weight,
    adapter_down_maps,
    adapter_up_maps,
    cotangent,
):
    model_width = section_layer_input.shape[2]
    sources = lax.axis_size("expert")
    flight = sources // SPLIT
    local_expert_group = lax.axis_index("expert") // SPLIT
    gate_proj = gate_weight[0]
    up_proj = up_weight[0]
    down_proj = down_weight[0]
    down_adapter_factor = adapter_down_maps[0]
    up_adapter_factor = lax.dynamic_index_in_dim(
        adapter_up_maps[0], local_expert_group, 0, keepdims=False
    )
    unit_count = gate_proj.shape[0]
    rank_width = down_adapter_factor.shape[1]
    reduce_over_rows = (((0,), (0,)), ((), ()))
    route_ids = token_expert_choice[0]
    onehot = (route_ids[:, :, None] == jnp.arange(flight, dtype=jnp.int32)).astype(jnp.int32)
    routed = onehot.sum(1)
    weight = (onehot * route_gate_steps[0][:, :, None]).sum(1).astype(jnp.float32) * LEVEL_STEP
    slot_index = jnp.cumsum(routed, axis=0) - routed
    placement = (slot_index[:, :, None] == jnp.arange(MOST, dtype=jnp.int32)) & (
        routed[:, :, None] > 0
    )
    place_half = placement.astype(jnp.bfloat16)
    place_full = placement.astype(jnp.float32)
    slot_gate = jnp.einsum("tfs,tf->fs", place_full, weight, precision=lax.Precision.HIGHEST)
    token_rows = jnp.einsum(
        "tfs,td->fsd", place_half, section_layer_input[0], preferred_element_type=jnp.float32
    ).astype(jnp.bfloat16)
    gradient_rows_local = jnp.einsum(
        "tfs,td->fsd", place_half, cotangent[0], preferred_element_type=jnp.float32
    )
    gradient_rows_local = (gradient_rows_local * slot_gate[:, :, None]).astype(jnp.bfloat16)
    send_tokens = jnp.repeat(token_rows, SPLIT, axis=0)
    send_grads = jnp.repeat(gradient_rows_local, SPLIT, axis=0)
    received = lax.all_to_all(send_tokens, "expert", split_axis=0, concat_axis=0, tiled=True)
    item_count = received.shape[1]
    pre_gate, pre_up, hidden, projected_hidden, layer_result_rows = expert_forward(
        received.reshape(-1, model_width),
        gate_proj,
        up_proj,
        down_proj,
        down_adapter_factor,
        up_adapter_factor,
    )
    returned = lax.all_to_all(
        layer_result_rows.reshape(sources, item_count, model_width),
        "expert",
        split_axis=0,
        concat_axis=0,
        tiled=True,
    )
    back_out, pre_gate, pre_up, hidden, projected_hidden = (
        returned,
        pre_gate.reshape(sources, item_count, unit_count),
        pre_up.reshape(sources, item_count, unit_count),
        hidden.reshape(sources, item_count, unit_count),
        projected_hidden.reshape(sources, item_count, rank_width),
    )
    recv_grads = lax.all_to_all(send_grads, "expert", split_axis=0, concat_axis=0, tiled=True)
    adapter_product, grad_input = expert_backward(
        recv_grads.reshape(-1, model_width),
        pre_gate.reshape(-1, unit_count),
        pre_up.reshape(-1, unit_count),
        gate_proj,
        up_proj,
        down_proj,
        down_adapter_factor,
        up_adapter_factor,
    )
    back_grad = lax.all_to_all(
        grad_input.reshape(sources, MOST, model_width),
        "expert",
        split_axis=0,
        concat_axis=0,
        tiled=True,
    )
    adapter_a_grad = lax.dot_general(
        hidden.reshape(-1, unit_count),
        adapter_product,
        reduce_over_rows,
        preferred_element_type=jnp.float32,
    )
    up_factor_partial = LOWRANK_SCALE * lax.dot_general(
        projected_hidden.reshape(-1, rank_width),
        recv_grads.reshape(-1, model_width),
        reduce_over_rows,
        preferred_element_type=jnp.float32,
    )
    b_spread = jnp.where(
        (jnp.arange(flight, dtype=jnp.int32) == local_expert_group)[:, None, None],
        up_factor_partial[None],
        jnp.zeros((), jnp.float32),
    )
    adapter_b_grad = lax.psum_scatter(b_spread, "expert", scatter_dimension=2, tiled=True)
    out_total = back_out.astype(jnp.float32).reshape(flight, SPLIT, MOST, model_width).sum(1)
    moe_out = jnp.einsum(
        "tfs,fsd->td", place_full * weight[:, :, None], out_total, precision=lax.Precision.HIGHEST
    ).astype(jnp.bfloat16)
    grad_total = back_grad.astype(jnp.float32).reshape(flight, SPLIT, MOST, model_width).sum(1)
    layer_grad = jnp.einsum(
        "tfs,fsd->td", place_full, grad_total, precision=lax.Precision.HIGHEST
    ).astype(jnp.bfloat16)
    next_input = from_behind(moe_out[None], "section", 1)
    prev_grad = from_behind(layer_grad[None], "section", -1)
    return (next_input, prev_grad, adapter_a_grad[None], adapter_b_grad[None])


def solution(mesh):
    placed = (
        P("section", "expert", None),
        P("section", "expert", None),
        P("section", "expert", None),
        P("section", "expert", None),
        P("section", "expert", None),
        P("section", "expert", None),
        P("section", "expert", None),
        P("section", None, None, None),
        P("section", "expert", None),
    )
    return jax.shard_map(
        on_device,
        mesh=mesh,
        in_specs=placed,
        out_specs=(
            P("section", "expert", None),
            P("section", "expert", None),
            P("section", "expert", None),
            P("section", None, None, "expert"),
        ),
        check_vma=False,
    )
```

profile of v0, /device:TPU:1, one launch (start us, length us, event | category | flops | bytes accessed | tf_op | source)
XLA Modules:
  0.0 231.4 jit_solution(9166179389941173448)
XLA Ops:
  11.5 7.6 %all-to-all-start = ((bf16[16,16,4096]{2,1,0:T(8,128)(2,1)}), bf16[16,16,4096]{2,1,0:T(8,128)(2,1)}, u32[]{:S(2)}, u32[]{:S(2)}) async-start(bf16[16,16,4096]{2,1,0:T(8,128)(2,1)} %bitcast.90), calls=%async_computation | async-start | bytes 4194304 | tf_op jit(solution)/shard_map/all_to_all | solution.py:117
  21.3 28.4 %all-to-all-done = bf16[16,16,4096]{2,1,0:T(8,128)(2,1)} async-done(((bf16[16,16,4096]{2,1,0:T(8,128)(2,1)}), bf16[16,16,4096]{2,1,0:T(8,128)(2,1)}, u32[]{:S(2)}, u32[]{:S(2)}) %all-to-all-start) | async-done | bytes 2097184 | tf_op jit(solution)/shard_map/all_to_all | solution.py:117
  51.3 4.4 %all-to-all-start.2 = ((bf16[16,16,4096]{2,1,0:T(8,128)(2,1)}), bf16[16,16,4096]{2,1,0:T(8,128)(2,1)}, u32[]{:S(2)}, u32[]{:S(2)}) async-start(bf16[16,16,4096]{2,1,0:T(8,128)(2,1)} %bitcast.89), calls=%async_computation.2 | async-start | bytes 4194304 | tf_op jit(solution)/shard_map/all_to_all | solution.py:141
  55.7 3.0 %fusion.17 = f32[256,256]{1,0:T(8,128)S(1)} fusion(bf16[256,4096]{1,0:T(8,128)(2,1)} %bitcast.5, bf16[1,256,4096]{2,1,0:T(8,128)(2,1)} %param.12), kind=kOutput, calls=%fused_computation.26 | convolution fusion | flops 536870912 | bytes 4456448 | tf_op jit(solution)/shard_map/dot_general | solution.py:22
  58.7 2.3 %multiply_convert_fusion.2 = (bf16[256,256]{1,0:T(8,128)(2,1)S(1)}, f32[256,256]{1,0:T(8,128)S(1)}) fusion(f32[256,256]{1,0:T(8,128)S(1)} %fusion.17, bf16[256,4096]{1,0:T(8,128)(2,1)} %bitcast.5, bf16[1,256,4096]{2,1,0:T(8,128)(2,1)S(1)} %copy-done), kind=kOutput, calls=%fused_computation.38 | convolution fusion | flops 537264128 | bytes 4849664 | tf_op jit(solution)/shard_map/dot_general | solution.py:25
  61.1 21.4 %all-to-all-done.2 = bf16[16,16,4096]{2,1,0:T(8,128)(2,1)} async-done(((bf16[16,16,4096]{2,1,0:T(8,128)(2,1)}), bf16[16,16,4096]{2,1,0:T(8,128)(2,1)}, u32[]{:S(2)}, u32[]{:S(2)}) %all-to-all-start.2) | async-done | bytes 2097184 | tf_op jit(solution)/shard_map/all_to_all | solution.py:141
  82.4 3.0 %fusion.8 = f32[256,256]{1,0:T(8,128)S(1)} fusion(bf16[256,4096]{1,0:T(8,128)(2,1)} %bitcast.22, bf16[1,256,4096]{2,1,0:T(8,128)(2,1)} %param.14), kind=kOutput, calls=%fused_computation.17 | convolution fusion | flops 536870912 | bytes 4456448 | tf_op jit(solution)/shard_map/dot_general | solution.py:54
  85.5 2.4 %fusion.19 = bf16[256,16]{0,1:T(8,128)(2,1)S(1)} fusion(bf16[256,4096]{1,0:T(8,128)(2,1)} %bitcast.22, bf16[1,4,16,4096]{3,2,1,0:T(8,128)(2,1)S(1)} %copy-done.2, s32[]{:T(128)S(6)} %select_n.14), kind=kOutput, calls=%fused_computation.31 | convolution fusion | flops 33562624 | bytes 2236420 | tf_op jit(solution)/shard_map/dot_general | solution.py:50
  88.9 2.2 fusion.2
  91.1 6.9 %all-to-all-start.3 = ((bf16[16,16,4096]{2,1,0:T(8,128)(2,1)}), bf16[16,16,4096]{2,1,0:T(8,128)(2,1)}, u32[]{:S(2)}, u32[]{:S(2)}) async-start(bf16[16,16,4096]{2,1,0:T(8,128)(2,1)} %bitcast.88), calls=%async_computation.3 | async-start | bytes 4194304 | tf_op jit(solution)/shard_map/all_to_all | solution.py:152
  98.2 2.3 %fusion.10 = f32[256,4096]{1,0:T(8,128)S(1)} fusion(bf16[256,256]{1,0:T(8,128)(2,1)S(1)} %get-tuple-element.6, bf16[1,256,4096]{2,1,0:T(8,128)(2,1)} %param.14), kind=kOutput, calls=%fused_computation.19 | convolution fusion | flops 536870912 | bytes 6422528 | tf_op jit(solution)/shard_map/dot_general | solution.py:30
  100.5 2.0 fusion.1
  102.6 22.0 %all-to-all-done.3 = bf16[16,16,4096]{2,1,0:T(8,128)(2,1)} async-done(((bf16[16,16,4096]{2,1,0:T(8,128)(2,1)}), bf16[16,16,4096]{2,1,0:T(8,128)(2,1)}, u32[]{:S(2)}, u32[]{:S(2)}) %all-to-all-start.3) | async-done | bytes 2097184 | tf_op jit(solution)/shard_map/all_to_all | solution.py:152
  124.6 7.2 %all-to-all-start.1 = ((bf16[16,16,4096]{2,1,0:T(8,128)(2,1)}), bf16[16,16,4096]{2,1,0:T(8,128)(2,1)}, u32[]{:S(2)}, u32[]{:S(2)}) async-start(bf16[16,16,4096]{2,1,0:T(8,128)(2,1)} %bitcast.91), calls=%async_computation.1 | async-start | bytes 4194304 | tf_op jit(solution)/shard_map/all_to_all | solution.py:127
  131.9 2.0 convolution_multiply_fusion.2
  135.0 2.1 convert_reduce_fusion
  137.0 2.0 fusion.5
  139.1 2.2 collective-permute-start.1
  141.3 17.2 %all-to-all-done.1 = bf16[16,16,4096]{2,1,0:T(8,128)(2,1)} async-done(((bf16[16,16,4096]{2,1,0:T(8,128)(2,1)}), bf16[16,16,4096]{2,1,0:T(8,128)(2,1)}, u32[]{:S(2)}, u32[]{:S(2)}) %all-to-all-start.1) | async-done | bytes 2097184 | tf_op jit(solution)/shard_map/all_to_all | solution.py:127
  158.5 2.1 convert_reduce_fusion.1
  162.4 6.4 %collective-permute-start = (bf16[1,128,4096]{2,1,0:T(8,128)(2,1)S(1)}, bf16[1,128,4096]{2,1,0:T(8,128)(2,1)}, u32[]{:S(2)}, u32[]{:S(2)}) collective-permute-start(bf16[1,128,4096]{2,1,0:T(8,128)(2,1)S(1)} %fusion.6), channel_id=1, source_target_pairs={{240,0},{0,16},{16,32},{32,48},{48,64},{64,80},{80,96},{96,112},{1... | collective-permute-start | bytes 3145736 | tf_op jit(solution)/shard_map/ppermute | solution.py:17
  169.6 11.0 %collective-permute-done = bf16[1,128,4096]{2,1,0:T(8,128)(2,1)} collective-permute-done((bf16[1,128,4096]{2,1,0:T(8,128)(2,1)S(1)}, bf16[1,128,4096]{2,1,0:T(8,128)(2,1)}, u32[]{:S(2)}, u32[]{:S(2)}) %collective-permute-start) | collective-permute-done | bytes 1048608 | tf_op jit(solution)/shard_map/ppermute | solution.py:17
  180.6 40.7 %reduce-scatter.2.cloned.1.call-done = f32[4,16,256]{2,1,0:T(8,128)} async-done(((f32[4,16,4096]{2,1,0:T(8,128)}), f32[4,16,256]{2,1,0:T(8,128)}) %reduce-scatter.2.cloned.1.call-update) | async-done | bytes 65552 | tf_op jit(solution)/shard_map/reduce_scatter | solution.py:176
  221.3 2.3 copy.24
  (35 shorter events, 13.9 us)
Async XLA Ops:
  7.2 51.5 %copy-start = (bf16[1,256,4096]{2,1,0:T(8,128)(2,1)S(1)}, bf16[1,256,4096]{2,1,0:T(8,128)(2,1)}, u32[]{:S(2)}) copy-start(bf16[1,256,4096]{2,1,0:T(8,128)(2,1)} %param.13) | copy-start | bytes 6291460
  11.5 38.2 %all-to-all-start = ((bf16[16,16,4096]{2,1,0:T(8,128)(2,1)}), bf16[16,16,4096]{2,1,0:T(8,128)(2,1)}, u32[]{:S(2)}, u32[]{:S(2)}) async-start(bf16[16,16,4096]{2,1,0:T(8,128)(2,1)} %bitcast.90), calls=%async_computation | async-start | bytes 4194304 | tf_op jit(solution)/shard_map/all_to_all | solution.py:117
  19.2 0.6 copy-start.4
  51.3 31.2 %all-to-all-start.2 = ((bf16[16,16,4096]{2,1,0:T(8,128)(2,1)}), bf16[16,16,4096]{2,1,0:T(8,128)(2,1)}, u32[]{:S(2)}, u32[]{:S(2)}) async-start(bf16[16,16,4096]{2,1,0:T(8,128)(2,1)} %bitcast.89), calls=%async_computation.2 | async-start | bytes 4194304 | tf_op jit(solution)/shard_map/all_to_all | solution.py:141
  82.4 3.0 %copy-start.2 = (bf16[1,4,16,4096]{3,2,1,0:T(8,128)(2,1)S(1)}, bf16[1,4,16,4096]{3,2,1,0:T(8,128)(2,1)}, u32[]{:S(2)}) copy-start(bf16[1,4,16,4096]{3,2,1,0:T(8,128)(2,1)} %param.16) | copy-start | bytes 1572868
  85.5 2.4 %copy-start.3 = (bf16[1,256,16]{1,2,0:T(8,128)(2,1)S(1)}, bf16[1,256,16]{1,2,0:T(8,128)(2,1)}, u32[]{:S(2)}) copy-start(bf16[1,256,16]{1,2,0:T(8,128)(2,1)} %param.15) | copy-start | bytes 24580
  85.5 2.7 %copy-start.1 = (bf16[1,256,4096]{2,1,0:T(8,128)(2,1)S(1)}, bf16[1,256,4096]{2,1,0:T(8,128)(2,1)}, u32[]{:S(2)}) copy-start(bf16[1,256,4096]{2,1,0:T(8,128)(2,1)} %param.12) | copy-start | bytes 6291460
  91.1 33.5 %all-to-all-start.3 = ((bf16[16,16,4096]{2,1,0:T(8,128)(2,1)}), bf16[16,16,4096]{2,1,0:T(8,128)(2,1)}, u32[]{:S(2)}, u32[]{:S(2)}) async-start(bf16[16,16,4096]{2,1,0:T(8,128)(2,1)} %bitcast.88), calls=%async_computation.3 | async-start | bytes 4194304 | tf_op jit(solution)/shard_map/all_to_all | solution.py:152
  124.6 33.9 %all-to-all-start.1 = ((bf16[16,16,4096]{2,1,0:T(8,128)(2,1)}), bf16[16,16,4096]{2,1,0:T(8,128)(2,1)}, u32[]{:S(2)}, u32[]{:S(2)}) async-start(bf16[16,16,4096]{2,1,0:T(8,128)(2,1)} %bitcast.91), calls=%async_computation.1 | async-start | bytes 4194304 | tf_op jit(solution)/shard_map/all_to_all | solution.py:127
  131.8 89.5 %reduce-scatter.2.cloned.1.call-start = ((), (), s32[]{:S(2)}) async-start(), calls=%async_computation.5 | async-start | bytes 1114112 | tf_op jit(solution)/shard_map/reduce_scatter | solution.py:176
  139.1 21.5 %copy-start.5 = (f32[128,4]{0,1:T(4,128)S(1)}, f32[128,4]{0,1:T(4,128)}, u32[]{:S(2)}) copy-start(f32[128,4]{0,1:T(4,128)} %copy-done.4) | copy-start | bytes 6148
  139.1 30.5 %collective-permute-start.1 = (bf16[1,128,4096]{2,1,0:T(8,128)(2,1)}, bf16[1,128,4096]{2,1,0:T(8,128)(2,1)S(1)}, u32[]{:S(2)}, u32[]{:S(2)}) collective-permute-start(bf16[1,128,4096]{2,1,0:T(8,128)(2,1)} %fusion.5), channel_id=1, source_target_pairs={{16,0},{32,16},{48,32},{64,48},{80,64},{96,80},{112,96},{128,112},... | collective-permute-start | bytes 3145736 | tf_op jit(solution)/shard_map/ppermute | solution.py:17
  162.4 18.2 %collective-permute-start = (bf16[1,128,4096]{2,1,0:T(8,128)(2,1)S(1)}, bf16[1,128,4096]{2,1,0:T(8,128)(2,1)}, u32[]{:S(2)}, u32[]{:S(2)}) collective-permute-start(bf16[1,128,4096]{2,1,0:T(8,128)(2,1)S(1)} %fusion.6), channel_id=1, source_target_pairs={{240,0},{0,16},{16,32},{32,48},{48,64},{64,80},{80,96},{96,112},{1... | collective-permute-start | bytes 3145736 | tf_op jit(solution)/shard_map/ppermute | solution.py:17
Sparse Core Ops, SparseCore 0:
  136.7 84.5 reduce-scatter.1
where the time goes:
time: 232 us; the launch traced here: 231 us
  waiting for transfers between devices  141 us (61%)
  starting transfers between devices  34.9 us (15%)
  matrix products  28.2 us (12%)
  between operations  14.2 us (6%)
  local copies, waits for them, and re-layouts  7.01 us (3%)
  other arithmetic  6.3 us (3%)
    reduce_scatter x1, waiting for transfers between devices, on_device(): lax.psum_scatter(b_spread, 'expert', scatter_dimension=2, tiled=True)  40.7 us
    all_to_all x1, waiting for transfers between devices, on_device(): lax.all_to_all(send_tokens, 'expert', split_axis=0, concat_axis=0, tiled=...  28.4 us
    all_to_all x1, waiting for transfers between devices, on_device(): lax.all_to_all(grad_input.reshape(sources, MOST, model_width), 'expert',...  22 us
    all_to_all x1, waiting for transfers between devices, on_device(): lax.all_to_all(send_grads, 'expert', split_axis=0, concat_axis=0, tiled=T...  21.4 us
    all_to_all x1, waiting for transfers between devices, on_device(): lax.all_to_all(layer_result_rows.reshape(sources, item_count, model_width...  17.2 us
    ppermute x2, waiting for transfers between devices, from_behind(): return lax.ppermute(block, axis, route)  11 us
    ppermute x2, starting transfers between devices, from_behind(): return lax.ppermute(block, axis, route)  8.61 us
    all_to_all x1, starting transfers between devices, on_device(): lax.all_to_all(send_tokens, 'expert', split_axis=0, concat_axis=0, tiled=...  7.64 us
  transfers between devices with their start and end apart: 7, of which 6 were waited for; matrix products, arithmetic and copies ran while one was open for 10% of the time, Pallas kernels for 0%

commit v1 on v0

v1 whole, which is shorter than its diff:
```python
import functools

import jax
import jax.numpy as jnp
from jax import lax
from jax.experimental import pallas as pl
from jax.experimental.pallas import tpu as pltpu
from jax.sharding import PartitionSpec as P

SPLIT = 4
MOST = 16
LOWRANK_SCALE = 2.0
LEVEL_STEP = 1.0 / 4096.0
F32 = jnp.float32
BF16 = jnp.bfloat16
FWD, BWD = 0, 1
LEFT, RIGHT = 0, 1


def dot_nt(a, b):
    return lax.dot_general(a, b, (((1,), (1,)), ((), ())), preferred_element_type=F32)


def dot_nn(a, b):
    return jnp.dot(a, b, preferred_element_type=F32)


def kernel(
    choice_ref, steps_ref, at_ref, tok_hbm, cot_hbm, wg_hbm, wu_hbm, wd_hbm, bup_hbm,
    out_hbm, grad_hbm, bg_hbm, ag_ref,
    rows_v, wg, wu, wd, bup, send, recv, pre_gate_v, pre_up_v, hid_v, lr_v,
    part, from_a, sum_b, from_b, fin, back, mix, mix_in, lat, lat_in, bsend, bg_v, out_v,
    load_sem, y_s, y_r, x1_s, x1_r, x2_s, x2_r, a_s, a_r, b_s, b_r, c_s, c_r,
    mix_s, mix_r, lat_s, lat_r, bg_s, bg_r, out_sem,
):
    half = recv.shape[-1]
    units = wg.shape[0]
    tokens = rows_v.shape[1]
    n_section = lax.axis_size("section")
    s = lax.axis_index("section")
    me = lax.axis_index("expert")
    y, x = me // SPLIT, me % SPLIT
    xr, xo, xl = (x + 1) % SPLIT, (x + 2) % SPLIT, (x + 3) % SPLIT
    s_next, s_prev = (s + 1) % n_section, (s + n_section - 1) % n_section

    def dev(row, col, sec=s):
        return {"section": sec, "expert": row * SPLIT + col}

    beside = (dev(y, xl), dev(y, xr))
    toward = (s_next, s_prev)

    def copy(src, dst, send_sem, recv_sem, device):
        return pltpu.make_async_remote_copy(
            src_ref=src, dst_ref=dst, send_sem=send_sem, recv_sem=recv_sem,
            device_id=device, device_id_type=pl.DeviceIdType.MESH,
        )

    def loop(first, last, body):
        def step(k, _):
            body(k)
            return 0
        lax.fori_loop(first, last, step, 0)

    loads = [
        pltpu.make_async_copy(src, dst, load_sem.at[i])
        for i, (src, dst) in enumerate((
            (tok_hbm, rows_v.at[FWD]), (cot_hbm, rows_v.at[BWD]), (wg_hbm, wg), (wu_hbm, wu),
            (wd_hbm, wd), (bup_hbm.at[y], bup),
        ))
    ]
    for load in loads:
        load.start()

    barrier = pltpu.get_barrier_semaphore()
    partners = [dev(y, xl), dev(y, xr), dev(y, xo)]
    partners += [dev((y + k) % SPLIT, x) for k in range(1, SPLIT)]
    partners += [dev((y + k) % SPLIT, x, sec) for k in range(SPLIT) for sec in toward]
    for device in partners:
        pl.semaphore_signal(barrier, inc=1, device_id=device, device_id_type=pl.DeviceIdType.MESH)

    shape = (SPLIT * MOST, tokens)
    row = lax.broadcasted_iota(jnp.int32, shape, 0)
    slot = row % MOST
    expert = (y + SPLIT - row // MOST) % SPLIT
    choice, steps = choice_ref[...], steps_ref[...]
    routed = jnp.zeros(shape, jnp.int32)
    gate = jnp.zeros(shape, jnp.int32)
    for j in range(choice.shape[0]):
        hit = choice[j:j + 1, :] == expert
        routed = jnp.where(hit, 1, routed)
        gate = jnp.where(hit, steps[j:j + 1, :], gate)
    square = (tokens, tokens)
    earlier = lax.broadcasted_iota(jnp.int32, square, 0) < lax.broadcasted_iota(jnp.int32, square, 1)
    taken = dot_nn(routed.astype(F32).astype(BF16), earlier.astype(F32).astype(BF16))
    placed = (routed > 0) & (taken == slot.astype(F32))
    place = jnp.where(placed, 1.0, 0.0).astype(F32)
    weight = place * (gate.astype(F32) * LEVEL_STEP)
    slot_gate = jnp.sum(weight, axis=1, keepdims=True)
    place_half = place.astype(BF16)

    def dispatch(ph):
        for h in range(2):
            out = dot_nn(place_half, rows_v[ph, :, h * half:(h + 1) * half])
            if ph == BWD:
                out = out * slot_gate
            out = out.astype(BF16)
            recv[ph, 0, h, pl.ds(x, 1)] = out[:MOST][None]
            for k in range(1, SPLIT):
                send[ph, k, h] = out[k * MOST:(k + 1) * MOST]

    def y_copy(ph, k, h):
        return copy(send.at[ph, k, h], recv.at[ph, k, h, x], y_s.at[ph, k, h], y_r.at[ph, k, h],
                    dev((y + SPLIT - k) % SPLIT, x))

    def x1_copy(ph, k, way, h, col):
        return copy(recv.at[ph, k, h, col], recv.at[ph, k, h, col], x1_s.at[ph, k, way, h],
                    x1_r.at[ph, k, way, h], beside[way])

    def x2_copy(ph, k, way, col):
        return copy(recv.at[ph, k, way, col], recv.at[ph, k, way, col], x2_s.at[ph, k, way],
                    x2_r.at[ph, k, way], beside[way])

    def x1_start(ph, k):
        for first in range(2):
            x1_copy(ph, k, LEFT, first, x).start()
            x1_copy(ph, k, RIGHT, 1 - first, x).start()

    def x2_start(ph, k):
        x1_copy(ph, k, LEFT, 0, xr).wait_recv()
        x2_copy(ph, k, LEFT, xr).start()
        x1_copy(ph, k, RIGHT, 1, xl).wait_recv()
        x2_copy(ph, k, RIGHT, xl).start()

    def gathered(ph, k):
        x1_copy(ph, k, LEFT, 1, xr).wait_recv()
        x1_copy(ph, k, RIGHT, 0, xl).wait_recv()
        x2_copy(ph, k, LEFT, xo).wait_recv()
        x2_copy(ph, k, RIGHT, xo).wait_recv()

    def y_wait(ph, k):
        for h in range(2):
            y_copy(ph, k, h).wait_recv()
        x1_start(ph, k)

    def a_copy(ph, k, way):
        return copy(part.at[ph, k, way, xo], from_a.at[ph, k, way], a_s.at[ph, k, way],
                    a_r.at[ph, k, way], beside[way])

    def b_copy(ph, k, way, late):
        src = sum_b.at[ph, k, way] if late else part.at[ph, k, 1 - way, (xl, xr)[way]]
        h = way if late else 1 - way
        return copy(src, from_b.at[ph, k, way, h], b_s.at[ph, k, way, h], b_r.at[ph, k, way, h],
                    beside[way])

    def parts_start(ph, k):
        for way in (LEFT, RIGHT):
            a_copy(ph, k, way).start()
        for way in (LEFT, RIGHT):
            b_copy(ph, k, way, False).start()

    def relay(ph, k):
        for way in (LEFT, RIGHT):
            a_copy(ph, k, way).wait_recv()
            mine = part[ph, k, way, pl.ds((xl, xr)[way], 1)][0].astype(F32)
            sum_b[ph, k, way] = (mine + from_a[ph, k, way].astype(F32)).astype(BF16)
            b_copy(ph, k, way, True).start()

    def c_copy(ph, k):
        return copy(fin.at[ph, k], back.at[ph, k], c_s.at[ph, k], c_r.at[ph, k],
                    dev((y + k) % SPLIT, x, toward[ph]))

    def finish(ph, k):
        for way in (LEFT, RIGHT):
            for late in (False, True):
                b_copy(ph, k, way, late).wait_recv()
        for h in range(2):
            total = part[ph, k, h, pl.ds(x, 1)][0].astype(F32)
            total = total + from_b[ph, k, LEFT, h].astype(F32) + from_b[ph, k, RIGHT, h].astype(F32)
            fin[ph, k, h] = total.astype(BF16)
        c_copy(ph, k).start()

    def rows_of(ph, k, h):
        return recv[ph, k, h].reshape(SPLIT * MOST, half)

    def forward(k):
        pre_gate = dot_nt(rows_of(FWD, k, 0), wg[:, :half]) + dot_nt(rows_of(FWD, k, 1), wg[:, half:])
        pre_up = dot_nt(rows_of(FWD, k, 0), wu[:, :half]) + dot_nt(rows_of(FWD, k, 1), wu[:, half:])
        hidden = (pre_gate * jax.nn.sigmoid(pre_gate) * pre_up).astype(BF16)
        pre_gate_v[k] = pre_gate
        pre_up_v[k] = pre_up
        hid_v[k] = hidden
        latent = dot_nt(hidden, at_ref[...]).astype(BF16)
        latent = (LOWRANK_SCALE * latent.astype(F32)).astype(BF16)
        for h in range(2):
            cols = slice(h * half, (h + 1) * half)
            out = dot_nn(hidden, wd[:, cols]) + dot_nn(latent, bup[:, cols])
            part[FWD, k, h] = out.astype(BF16).reshape(SPLIT, MOST, half)

    def backward(k):
        low = dot_nt(rows_of(BWD, k, 0), bup[:, :half]) + dot_nt(rows_of(BWD, k, 1), bup[:, half:])
        low = (LOWRANK_SCALE * low).astype(BF16)
        lr_v[k] = low
        grad_hidden = dot_nt(rows_of(BWD, k, 0), wd[:, :half]) + dot_nt(rows_of(BWD, k, 1), wd[:, half:])
        grad_hidden = grad_hidden + dot_nn(low, at_ref[...])
        pre_gate, pre_up = pre_gate_v[k], pre_up_v[k]
        sig = jax.nn.sigmoid(pre_gate)
        grad_gate = (grad_hidden * pre_up * sig * (1.0 + pre_gate * (1.0 - sig))).astype(BF16)
        grad_up = (grad_hidden * pre_gate * sig).astype(BF16)
        for h in range(2):
            cols = slice(h * half, (h + 1) * half)
            out = dot_nn(grad_gate, wg[:, cols]) + dot_nn(grad_up, wu[:, cols])
            part[BWD, k, h] = out.astype(BF16).reshape(SPLIT, MOST, half)

    loads[0].wait()
    dispatch(FWD)
    pl.semaphore_wait(barrier, len(partners))
    x1_start(FWD, 0)
    for k in (1, 3, 2):
        for h in range(2):
            y_copy(FWD, k, h).start()

    loads[1].wait()
    dispatch(BWD)
    x1_start(BWD, 0)
    for k in (1, 3, 2):
        for h in range(2):
            y_copy(BWD, k, h).start()

    high = weight.astype(BF16).astype(F32)
    mixes = (jnp.concatenate([high, weight - high], axis=0),
             jnp.concatenate([place, jnp.zeros_like(place)], axis=0))
    for ph in (FWD, BWD):
        mix[ph] = jnp.transpose(mixes[ph]).astype(BF16)

    def mix_copy(ph):
        return copy(mix.at[ph], mix_in.at[ph], mix_s.at[ph], mix_r.at[ph], dev(y, x, toward[ph]))

    for ph in (FWD, BWD):
        mix_copy(ph).start()

    loop(1, SPLIT, lambda k: y_wait(FWD, k))
    loop(1, SPLIT, lambda k: y_wait(BWD, k))
    loop(0, SPLIT, lambda k: x2_start(FWD, k))
    for load in loads[2:]:
        load.wait()

    def forward_step(k):
        gathered(FWD, k)
        forward(k)
        parts_start(FWD, k)
        x2_start(BWD, k)

    loop(0, SPLIT, forward_step)

    hidden_all = hid_v[...].reshape(SPLIT * SPLIT * MOST, units)
    lat[...] = dot_nt(at_ref[...], hidden_all).astype(BF16)

    def lat_copy(i):
        return copy(lat, lat_in.at[i], lat_s.at[i], lat_r.at[i],
                    (dev(y, xl), dev(y, xr), dev(y, xo))[i])

    for i in range(3):
        lat_copy(i).start()

    def backward_step(k):
        gathered(BWD, k)
        backward(k)
        parts_start(BWD, k)
        relay(FWD, k)

    loop(0, SPLIT, backward_step)

    ag_ref[...] = lax.dot_general(
        lr_v[...].reshape(SPLIT * SPLIT * MOST, lr_v.shape[-1]),
        hid_v[...].reshape(SPLIT * SPLIT * MOST, units),
        (((0,), (0,)), ((), ())), preferred_element_type=F32)

    def middle_step(k):
        relay(BWD, k)
        finish(FWD, k)

    loop(0, SPLIT, middle_step)

    width = bg_v.shape[-1]
    lat_sum = lat[...].astype(F32)
    for i in range(3):
        lat_copy(i).wait_recv()
        lat_sum = lat_sum + lat_in[i].astype(F32)
    lat_sum = LOWRANK_SCALE * lat_sum
    lat_high = lat_sum.astype(BF16)
    lat_low = (lat_sum - lat_high.astype(F32)).astype(BF16)

    def bg_copy(k):
        return copy(bsend.at[k], bg_v.at[y], bg_s.at[k], bg_r.at[k], dev((y + k) % SPLIT, x))

    def bg_wait(k):
        return copy(bsend.at[k], bg_v.at[(y + SPLIT - k) % SPLIT], bg_s.at[k], bg_r.at[k],
                    dev((y + k) % SPLIT, x))

    per_half = half // width
    for k in range(SPLIT):
        block = ((y + k) % SPLIT) * SPLIT + x
        cols = pl.ds(pl.multiple_of((block % per_half) * width, width), width)
        grad_rows = recv[BWD, :, pl.ds(block // per_half, 1), :, :, cols]
        grad_rows = grad_rows.reshape(SPLIT * SPLIT * MOST, width)
        value = dot_nn(lat_high, grad_rows) + dot_nn(lat_low, grad_rows)
        if k == 0:
            bg_v[pl.ds(y, 1)] = value[None]
        else:
            bsend[k] = value
            bg_copy(k).start()

    tile = min(512, half)

    def out_copy(ph, h, n):
        cols = slice(h * half + n * tile, h * half + (n + 1) * tile)
        return pltpu.make_async_copy(
            out_v.at[ph, :, cols], (out_hbm, grad_hbm)[ph].at[:, cols],
            out_sem.at[ph, h * (half // tile) + n])

    def combine(ph):
        mix_copy(ph).wait_recv()
        for k in range(SPLIT):
            c_copy(ph, k).wait_recv()
        spread = mix_in[ph]
        for h in range(2):
            for n in range(half // tile):
                block = back[ph, :, h, :, n * tile:(n + 1) * tile].reshape(SPLIT * MOST, tile)
                block = jnp.concatenate([block, block], axis=0)
                cols = slice(h * half + n * tile, h * half + (n + 1) * tile)
                out_v[ph, :, cols] = dot_nn(spread, block).astype(BF16)
                out_copy(ph, h, n).start()

    loop(0, SPLIT - 1, lambda k: finish(BWD, k))
    combine(FWD)
    finish(BWD, SPLIT - 1)
    for k in range(1, SPLIT):
        bg_wait(k).wait_recv()
    bg_out = pltpu.make_async_copy(bg_v, bg_hbm, load_sem.at[0])
    bg_out.start()
    combine(BWD)

    bg_out.wait()
    for ph in (FWD, BWD):
        mix_copy(ph).wait_send()
    for i in range(3):
        lat_copy(i).wait_send()
    for k in range(1, SPLIT):
        bg_copy(k).wait_send()

    def sent(k):
        for ph in (FWD, BWD):
            for way in (LEFT, RIGHT):
                for h in range(2):
                    x1_copy(ph, k, way, h, x).wait_send()
                    b_copy(ph, k, way, h == way).wait_send()
                x2_copy(ph, k, way, x).wait_send()
                a_copy(ph, k, way).wait_send()
            c_copy(ph, k).wait_send()

    loop(0, SPLIT, sent)

    def y_sent(k):
        for ph in (FWD, BWD):
            for h in range(2):
                y_copy(ph, k, h).wait_send()

    loop(1, SPLIT, y_sent)
    for ph in (FWD, BWD):
        for h in range(2):
            for n in range(half // tile):
                out_copy(ph, h, n).wait()


def on_device(
    section_layer_input, token_expert_choice, route_gate_steps, gate_weight, up_weight, down_weight,
    adapter_down_maps, adapter_up_maps, cotangent,
):
    tokens, width = section_layer_input.shape[1:]
    units = gate_weight.shape[1]
    rank = adapter_down_maps.shape[2]
    half = width // 2
    cols = width // lax.axis_size("expert")
    dma = pltpu.SemaphoreType.DMA
    flight = SPLIT * MOST
    tile = min(512, half)
    anywhere = pl.BlockSpec(memory_space=pl.ANY)
    vmem = pl.BlockSpec(memory_space=pltpu.VMEM)
    out, grad, b_grad, a_grad = pl.pallas_call(
        kernel,
        out_shape=(
            jax.ShapeDtypeStruct((tokens, width), BF16),
            jax.ShapeDtypeStruct((tokens, width), BF16),
            jax.ShapeDtypeStruct((SPLIT, rank, cols), F32),
            jax.ShapeDtypeStruct((rank, units), F32),
        ),
        in_specs=[vmem] * 3 + [anywhere] * 6,
        out_specs=(anywhere, anywhere, anywhere, vmem),
        scratch_shapes=[
            pltpu.VMEM((2, tokens, width), BF16),
            pltpu.VMEM((units, width), BF16),
            pltpu.VMEM((units, width), BF16),
            pltpu.VMEM((units, width), BF16),
            pltpu.VMEM((rank, width), BF16),
            pltpu.VMEM((2, SPLIT, 2, MOST, half), BF16),
            pltpu.VMEM((2, SPLIT, 2, SPLIT, MOST, half), BF16),
            pltpu.VMEM((SPLIT, flight, units), F32),
            pltpu.VMEM((SPLIT, flight, units), F32),
            pltpu.VMEM((SPLIT, flight, units), BF16),
            pltpu.VMEM((SPLIT, flight, rank), BF16),
            pltpu.VMEM((2, SPLIT, 2, SPLIT, MOST, half), BF16),
            pltpu.VMEM((2, SPLIT, 2, MOST, half), BF16),
            pltpu.VMEM((2, SPLIT, 2, MOST, half), BF16),
            pltpu.VMEM((2, SPLIT, 2, 2, MOST, half), BF16),
            pltpu.VMEM((2, SPLIT, 2, MOST, half), BF16),
            pltpu.VMEM((2, SPLIT, 2, MOST, half), BF16),
            pltpu.VMEM((2, tokens, 2 * flight), BF16),
            pltpu.VMEM((2, tokens, 2 * flight), BF16),
            pltpu.VMEM((rank, SPLIT * flight), BF16),
            pltpu.VMEM((3, rank, SPLIT * flight), BF16),
            pltpu.VMEM((SPLIT, rank, cols), F32),
            pltpu.VMEM((SPLIT, rank, cols), F32),
            pltpu.VMEM((2, tokens, width), BF16),
            dma((6,)),
            dma((2, SPLIT, 2)), dma((2, SPLIT, 2)),
            dma((2, SPLIT, 2, 2)), dma((2, SPLIT, 2, 2)),
            dma((2, SPLIT, 2)), dma((2, SPLIT, 2)),
            dma((2, SPLIT, 2)), dma((2, SPLIT, 2)),
            dma((2, SPLIT, 2, 2)), dma((2, SPLIT, 2, 2)),
            dma((2, SPLIT)), dma((2, SPLIT)),
            dma((2,)), dma((2,)),
            dma((3,)), dma((3,)),
            dma((SPLIT,)), dma((SPLIT,)),
            dma((2, 2 * (half // tile))),
        ],
        compiler_params=pltpu.CompilerParams(
            collective_id=0, has_side_effects=True, vmem_limit_bytes=48 * 1024 * 1024),
    )(
        token_expert_choice[0].T, route_gate_steps[0].T, adapter_down_maps[0].T,
        section_layer_input[0], cotangent[0], gate_weight[0], up_weight[0], down_weight[0],
        adapter_up_maps[0],
    )
    return out[None], grad[None], a_grad.T[None], b_grad[None]


def solution(mesh):
    tokens = P("section", "expert", None)
    return jax.shard_map(
        on_device,
        mesh=mesh,
        in_specs=(tokens,) * 7 + (P("section", None, None, None), tokens),
        out_specs=(tokens, tokens, tokens, P("section", None, None, "expert")),
        check_vma=False,
    )
```

time: 232 us -> 100 us (0.43)
  the two profiles are of different devices: /device:TPU:1 before, /device:TPU:8 now
where the time goes in v1:
time: 100 us
  Pallas kernels  90.6 us (91%)
  local copies, waits for them, and re-layouts  8.73 us (9%)
    pallas_call x1, Pallas kernels, on_device(): pl.pallas_call(kernel, out_shape=(jax.ShapeDtypeStruct((tokens, width), B...  90.6 us
    unnamed x16, local copies, waits for them, and re-layouts  8.73 us

profile of v1, /device:TPU:8, one launch (start us, length us, event | category | flops | bytes accessed | tf_op | source)
XLA Modules:
  0.0 100.0 jit_solution(17595012671013367000)
XLA Ops:
  0.6 0.0 copy-start
  0.6 1.2 %copy-done = bf16[1,128,4096]{2,1,0:T(8,128)(2,1)S(1)} copy-done((bf16[1,128,4096]{2,1,0:T(8,128)(2,1)S(1)}, bf16[1,128,4096]{2,1,0:T(8,128)(2,1)}, u32[]{:S(2)}) %copy-start) | copy-done | bytes 1048600
  1.9 0.0 copy-start.1
  1.9 1.2 %copy-done.1 = bf16[1,128,4096]{2,1,0:T(8,128)(2,1)S(1)} copy-done((bf16[1,128,4096]{2,1,0:T(8,128)(2,1)S(1)}, bf16[1,128,4096]{2,1,0:T(8,128)(2,1)}, u32[]{:S(2)}) %copy-start.1) | copy-done | bytes 1048600
  3.1 0.0 copy-start.2
  3.1 1.0 %copy-done.2 = bf16[1,4,16,4096]{3,2,1,0:T(8,128)(2,1)S(1)} copy-done((bf16[1,4,16,4096]{3,2,1,0:T(8,128)(2,1)S(1)}, bf16[1,4,16,4096]{3,2,1,0:T(8,128)(2,1)}, u32[]{:S(2)}) %copy-start.2) | copy-done | bytes 524312
  4.1 0.0 copy-start.3
  4.1 0.7 copy-done.3
  4.8 0.0 copy-start.4
  4.8 0.7 copy-done.4
  5.5 0.0 copy-start.5
  5.5 0.7 copy-done.5
  6.2 90.6 %shard_map.120 = (bf16[128,4096]{1,0:T(8,128)(2,1)S(1)}, bf16[128,4096]{1,0:T(8,128)(2,1)S(1)}, f32[4,16,256]{2,1,0:T(8,128)S(1)}, f32[16,256]{1,0:T(8,128)S(1)}) custom-call(s32[8,128]{1,0:T(8,128)S(1)} %bitcast.29, s32[8,128]{1,0:T(8,128)S(1)} %bitcast.30, bf16[16,256]{1,0:T(8,128)(2,1)S(1)} %bitcast.28, bf16[128,4096]{1,0:T(8,128)(2,1)S(1)} %bitcast.21, ...), custom_call_target="tpu_custom_call" | custom-call | tf_op jit(solution)/shard_map/pallas_call | solution.py:389
  96.8 1.0 copy.17
  97.8 1.0 copy.18
  98.7 0.6 copy.19
  99.3 0.6 copy.20
Async XLA Ops:
  0.6 1.2 %copy-start = (bf16[1,128,4096]{2,1,0:T(8,128)(2,1)S(1)}, bf16[1,128,4096]{2,1,0:T(8,128)(2,1)}, u32[]{:S(2)}) copy-start(bf16[1,128,4096]{2,1,0:T(8,128)(2,1)} %param.9) | copy-start | bytes 3145732
  1.9 1.2 %copy-start.1 = (bf16[1,128,4096]{2,1,0:T(8,128)(2,1)S(1)}, bf16[1,128,4096]{2,1,0:T(8,128)(2,1)}, u32[]{:S(2)}) copy-start(bf16[1,128,4096]{2,1,0:T(8,128)(2,1)} %param.17) | copy-start | bytes 3145732
  3.1 1.0 %copy-start.2 = (bf16[1,4,16,4096]{3,2,1,0:T(8,128)(2,1)S(1)}, bf16[1,4,16,4096]{3,2,1,0:T(8,128)(2,1)}, u32[]{:S(2)}) copy-start(bf16[1,4,16,4096]{3,2,1,0:T(8,128)(2,1)} %param.16) | copy-start | bytes 1572868
  4.1 0.7 copy-start.3
  4.8 0.7 copy-start.4
  5.5 0.7 copy-start.5

commit v2 on v1

--- a/solution.py
+++ b/solution.py
@@ -26,12 +26,12 @@
 
 
 def kernel(
-    choice_ref, steps_ref, at_ref, tok_hbm, cot_hbm, wg_hbm, wu_hbm, wd_hbm, bup_hbm,
-    out_hbm, grad_hbm, bg_hbm, ag_ref,
+    choice_hbm, steps_hbm, at_hbm, tok_hbm, cot_hbm, wg_hbm, wu_hbm, wd_hbm, bup_hbm,
+    out_v, back_g, mix_g, bg_v, ag_ref,
     rows_v, wg, wu, wd, bup, send, recv, pre_gate_v, pre_up_v, hid_v, lr_v,
-    part, from_a, sum_b, from_b, fin, back, mix, mix_in, lat, lat_in, bsend, bg_v, out_v,
+    part, from_a, sum_b, from_b, fin, back_f, mix, mix_f, lat, lat_in, bsend, choice_v, steps_v, at_v,
     load_sem, y_s, y_r, x1_s, x1_r, x2_s, x2_r, a_s, a_r, b_s, b_r, c_s, c_r,
-    mix_s, mix_r, lat_s, lat_r, bg_s, bg_r, out_sem,
+    mix_s, mix_r, lat_s, lat_r, bg_s, bg_r,
 ):
     half = recv.shape[-1]
     units = wg.shape[0]
@@ -64,8 +64,9 @@
     loads = [
         pltpu.make_async_copy(src, dst, load_sem.at[i])
         for i, (src, dst) in enumerate((
-            (tok_hbm, rows_v.at[FWD]), (cot_hbm, rows_v.at[BWD]), (wg_hbm, wg), (wu_hbm, wu),
-            (wd_hbm, wd), (bup_hbm.at[y], bup),
+            (choice_hbm, choice_v), (steps_hbm, steps_v), (tok_hbm, rows_v.at[FWD]),
+            (cot_hbm, rows_v.at[BWD]), (at_hbm, at_v), (wg_hbm, wg), (wu_hbm, wu), (wd_hbm, wd),
+            (bup_hbm.at[y], bup),
         ))
     ]
     for load in loads:
@@ -82,7 +83,9 @@
     row = lax.broadcasted_iota(jnp.int32, shape, 0)
     slot = row % MOST
     expert = (y + SPLIT - row // MOST) % SPLIT
-    choice, steps = choice_ref[...], steps_ref[...]
+    loads[0].wait()
+    loads[1].wait()
+    choice, steps = choice_v[...], steps_v[...]
     routed = jnp.zeros(shape, jnp.int32)
     gate = jnp.zeros(shape, jnp.int32)
     for j in range(choice.shape[0]):
@@ -166,7 +169,7 @@
             b_copy(ph, k, way, True).start()
 
     def c_copy(ph, k):
-        return copy(fin.at[ph, k], back.at[ph, k], c_s.at[ph, k], c_r.at[ph, k],
+        return copy(fin.at[ph, k], (back_f, back_g)[ph].at[k], c_s.at[ph, k], c_r.at[ph, k],
                     dev((y + k) % SPLIT, x, toward[ph]))
 
     def finish(ph, k):
@@ -189,7 +192,7 @@
         pre_gate_v[k] = pre_gate
         pre_up_v[k] = pre_up
         hid_v[k] = hidden
-        latent = dot_nt(hidden, at_ref[...]).astype(BF16)
+        latent = dot_nt(hidden, at_v[...]).astype(BF16)
         latent = (LOWRANK_SCALE * latent.astype(F32)).astype(BF16)
         for h in range(2):
             cols = slice(h * half, (h + 1) * half)
@@ -201,7 +204,7 @@
         low = (LOWRANK_SCALE * low).astype(BF16)
         lr_v[k] = low
         grad_hidden = dot_nt(rows_of(BWD, k, 0), wd[:, :half]) + dot_nt(rows_of(BWD, k, 1), wd[:, half:])
-        grad_hidden = grad_hidden + dot_nn(low, at_ref[...])
+        grad_hidden = grad_hidden + dot_nn(low, at_v[...])
         pre_gate, pre_up = pre_gate_v[k], pre_up_v[k]
         sig = jax.nn.sigmoid(pre_gate)
         grad_gate = (grad_hidden * pre_up * sig * (1.0 + pre_gate * (1.0 - sig))).astype(BF16)
@@ -211,7 +214,7 @@
             out = dot_nn(grad_gate, wg[:, cols]) + dot_nn(grad_up, wu[:, cols])
             part[BWD, k, h] = out.astype(BF16).reshape(SPLIT, MOST, half)
 
-    loads[0].wait()
+    loads[2].wait()
     dispatch(FWD)
     pl.semaphore_wait(barrier, len(partners))
     x1_start(FWD, 0)
@@ -219,7 +222,7 @@
         for h in range(2):
             y_copy(FWD, k, h).start()
 
-    loads[1].wait()
+    loads[3].wait()
     dispatch(BWD)
     x1_start(BWD, 0)
     for k in (1, 3, 2):
@@ -233,7 +236,7 @@
         mix[ph] = jnp.transpose(mixes[ph]).astype(BF16)
 
     def mix_copy(ph):
-        return copy(mix.at[ph], mix_in.at[ph], mix_s.at[ph], mix_r.at[ph], dev(y, x, toward[ph]))
+        return copy(mix.at[ph], (mix_f, mix_g)[ph], mix_s.at[ph], mix_r.at[ph], dev(y, x, toward[ph]))
 
     for ph in (FWD, BWD):
         mix_copy(ph).start()
@@ -241,7 +244,7 @@
     loop(1, SPLIT, lambda k: y_wait(FWD, k))
     loop(1, SPLIT, lambda k: y_wait(BWD, k))
     loop(0, SPLIT, lambda k: x2_start(FWD, k))
-    for load in loads[2:]:
+    for load in loads[4:]:
         load.wait()
 
     def forward_step(k):
@@ -253,7 +256,7 @@
     loop(0, SPLIT, forward_step)
 
     hidden_all = hid_v[...].reshape(SPLIT * SPLIT * MOST, units)
-    lat[...] = dot_nt(at_ref[...], hidden_all).astype(BF16)
+    lat[...] = dot_nt(at_v[...], hidden_all).astype(BF16)
 
     def lat_copy(i):
         return copy(lat, lat_in.at[i], lat_s.at[i], lat_r.at[i],
@@ -310,37 +313,20 @@
             bsend[k] = value
             bg_copy(k).start()
 
-    tile = min(512, half)
-
-    def out_copy(ph, h, n):
-        cols = slice(h * half + n * tile, h * half + (n + 1) * tile)
-        return pltpu.make_async_copy(
-            out_v.at[ph, :, cols], (out_hbm, grad_hbm)[ph].at[:, cols],
-            out_sem.at[ph, h * (half // tile) + n])
-
-    def combine(ph):
+    def arrived(ph):
         mix_copy(ph).wait_recv()
         for k in range(SPLIT):
             c_copy(ph, k).wait_recv()
-        spread = mix_in[ph]
-        for h in range(2):
-            for n in range(half // tile):
-                block = back[ph, :, h, :, n * tile:(n + 1) * tile].reshape(SPLIT * MOST, tile)
-                block = jnp.concatenate([block, block], axis=0)
-                cols = slice(h * half + n * tile, h * half + (n + 1) * tile)
-                out_v[ph, :, cols] = dot_nn(spread, block).astype(BF16)
-                out_copy(ph, h, n).start()
 
     loop(0, SPLIT - 1, lambda k: finish(BWD, k))
-    combine(FWD)
+    arrived(FWD)
+    for cols, value in spread(mix_f, back_f):
+        out_v[:, cols] = value
     finish(BWD, SPLIT - 1)
     for k in range(1, SPLIT):
         bg_wait(k).wait_recv()
-    bg_out = pltpu.make_async_copy(bg_v, bg_hbm, load_sem.at[0])
-    bg_out.start()
-    combine(BWD)
-
-    bg_out.wait()
+    arrived(BWD)
+
     for ph in (FWD, BWD):
         mix_copy(ph).wait_send()
     for i in range(3):
@@ -366,10 +352,31 @@
                 y_copy(ph, k, h).wait_send()
 
     loop(1, SPLIT, y_sent)
-    for ph in (FWD, BWD):
-        for h in range(2):
-            for n in range(half // tile):
-                out_copy(ph, h, n).wait()
+
+
+def spread(mix, rows):
+    half = rows.shape[-1]
+    tile = min(512, half)
+    for h in range(2):
+        for n in range(0, half, tile):
+            block = rows[:, h, :, n:n + tile].reshape(SPLIT * MOST, tile)
+            block = jnp.concatenate([block, block], axis=0)
+            yield slice(h * half + n, h * half + n + tile), dot_nn(mix[...], block).astype(BF16)
+
+
+def last_kernel(
+    out_v, back_g, mix_g, bg_v, ag_v, out_hbm, grad_hbm, bg_hbm, ag_hbm, grad_v, sem, grad_sem
+):
+    pairs = ((out_v, out_hbm), (bg_v, bg_hbm), (ag_v, ag_hbm))
+    copies = [pltpu.make_async_copy(src, dst, sem.at[i]) for i, (src, dst) in enumerate(pairs)]
+    for copy in copies:
+        copy.start()
+    for i, (cols, value) in enumerate(spread(mix_g, back_g)):
+        grad_v[:, cols] = value
+        copies.append(pltpu.make_async_copy(grad_v.at[:, cols], grad_hbm.at[:, cols], grad_sem.at[i]))
+        copies[-1].start()
+    for copy in copies:
+        copy.wait()
 
 
 def on_device(
@@ -383,19 +390,20 @@
     cols = width // lax.axis_size("expert")
     dma = pltpu.SemaphoreType.DMA
     flight = SPLIT * MOST
-    tile = min(512, half)
-    anywhere = pl.BlockSpec(memory_space=pl.ANY)
+    tiles = width // min(512, half)
+    hbm = pl.BlockSpec(memory_space=pltpu.HBM)
     vmem = pl.BlockSpec(memory_space=pltpu.VMEM)
-    out, grad, b_grad, a_grad = pl.pallas_call(
+    held = pl.pallas_call(
         kernel,
         out_shape=(
             jax.ShapeDtypeStruct((tokens, width), BF16),
-            jax.ShapeDtypeStruct((tokens, width), BF16),
+            jax.ShapeDtypeStruct((SPLIT, 2, MOST, half), BF16),
+            jax.ShapeDtypeStruct((tokens, 2 * flight), BF16),
             jax.ShapeDtypeStruct((SPLIT, rank, cols), F32),
             jax.ShapeDtypeStruct((rank, units), F32),
         ),
-        in_specs=[vmem] * 3 + [anywhere] * 6,
-        out_specs=(anywhere, anywhere, anywhere, vmem),
+        in_specs=[hbm] * 9,
+        out_specs=(vmem,) * 5,
         scratch_shapes=[
             pltpu.VMEM((2, tokens, width), BF16),
             pltpu.VMEM((units, width), BF16),
@@ -413,15 +421,16 @@
             pltpu.VMEM((2, SPLIT, 2, MOST, half), BF16),
             pltpu.VMEM((2, SPLIT, 2, 2, MOST, half), BF16),
             pltpu.VMEM((2, SPLIT, 2, MOST, half), BF16),
-            pltpu.VMEM((2, SPLIT, 2, MOST, half), BF16),
+            pltpu.VMEM((SPLIT, 2, MOST, half), BF16),
             pltpu.VMEM((2, tokens, 2 * flight), BF16),
-            pltpu.VMEM((2, tokens, 2 * flight), BF16),
+            pltpu.VMEM((tokens, 2 * flight), BF16),
             pltpu.VMEM((rank, SPLIT * flight), BF16),
             pltpu.VMEM((3, rank, SPLIT * flight), BF16),
             pltpu.VMEM((SPLIT, rank, cols), F32),
-            pltpu.VMEM((SPLIT, rank, cols), F32),
-            pltpu.VMEM((2, tokens, width), BF16),
-            dma((6,)),
+            pltpu.VMEM(token_expert_choice.shape[:0:-1], jnp.int32),
+            pltpu.VMEM(token_expert_choice.shape[:0:-1], jnp.int32),
+            pltpu.VMEM((rank, units), BF16),
+            dma((9,)),
             dma((2, SPLIT, 2)), dma((2, SPLIT, 2)),
             dma((2, SPLIT, 2, 2)), dma((2, SPLIT, 2, 2)),
             dma((2, SPLIT, 2)), dma((2, SPLIT, 2)),
@@ -431,15 +440,27 @@
             dma((2,)), dma((2,)),
             dma((3,)), dma((3,)),
             dma((SPLIT,)), dma((SPLIT,)),
-            dma((2, 2 * (half // tile))),
         ],
         compiler_params=pltpu.CompilerParams(
             collective_id=0, has_side_effects=True, vmem_limit_bytes=48 * 1024 * 1024),
     )(
-        token_expert_choice[0].T, route_gate_steps[0].T, adapter_down_maps[0].T,
+        *[pltpu.with_memory_space_constraint(a, pltpu.HBM) for a in (token_expert_choice[0].T, route_gate_steps[0].T, adapter_down_maps[0].T,
         section_layer_input[0], cotangent[0], gate_weight[0], up_weight[0], down_weight[0],
-        adapter_up_maps[0],
+        adapter_up_maps[0])],
     )
+    out, grad, b_grad, a_grad = pl.pallas_call(
+        last_kernel,
+        out_shape=(
+            jax.ShapeDtypeStruct((tokens, width), BF16),
+            jax.ShapeDtypeStruct((tokens, width), BF16),
+            jax.ShapeDtypeStruct((SPLIT, rank, cols), F32),
+            jax.ShapeDtypeStruct((rank, units), F32),
+        ),
+        in_specs=[vmem] * 5,
+        out_specs=(hbm,) * 4,
+        scratch_shapes=[pltpu.VMEM((tokens, width), BF16), dma((3,)), dma((tiles,))],
+        compiler_params=pltpu.CompilerParams(vmem_limit_bytes=16 * 1024 * 1024),
+    )(*held)
     return out[None], grad[None], a_grad.T[None], b_grad[None]
 
 

time: 100 us -> 89.8 us (0.90)
  the two profiles are of different devices: /device:TPU:8 before, /device:TPU:1 now
where the time goes in v2:
time: 89.8 us; the launch traced here: 88.7 us
  Pallas kernels  88.1 us (98%)
    pallas_call x1, Pallas kernels, on_device(): pl.pallas_call(kernel, out_shape=(jax.ShapeDtypeStruct((tokens, width), B...  86.7 us

profile of v2, /device:TPU:1, one launch (start us, length us, event | category | flops | bytes accessed | tf_op | source)
XLA Modules:
  0.0 88.7 jit_solution(12276690108223670270)
XLA Ops:
  0.6 86.7 %shard_map.120 = (bf16[128,4096]{1,0:T(8,128)(2,1)S(1)}, bf16[4,2,16,2048]{3,2,1,0:T(8,128)(2,1)S(1)}, bf16[128,128]{1,0:T(8,128)(2,1)S(1)}, f32[4,16,256]{2,1,0:T(8,128)S(1)}, f32[16,256]{1,0:T(8,128)S(1)}) custom-call(s32[8,128]{1,0:T(8,128)} %bitcast.28, s32[8,128]{1,0:T(8,128)} %bitcast.29, bf16[16,256]{1,0:T(8,128)(2,1)} %bitcast.27, ...), custom_call_target="tpu_custom_call" | custom-call | tf_op jit(solution)/shard_map/pallas_call | solution.py:396
  87.3 1.4 %shard_map.121 = (bf16[128,4096]{1,0:T(8,128)(2,1)}, bf16[128,4096]{1,0:T(8,128)(2,1)}, f32[4,16,256]{2,1,0:T(8,128)}, f32[16,256]{1,0:T(8,128)}) custom-call(bf16[128,4096]{1,0:T(8,128)(2,1)S(1)} %get-tuple-element.13.out_v, bf16[4,2,16,2048]{3,2,1,0:T(8,128)(2,1)S(1)} %get-tuple-element.14.back_g, bf16[128,128]{1,0:T(8,128)(2,1)S(1)} %get-tuple-element.15.mix_g, ...), custom_call_target="tpu_custom_call" | custom-call | tf_op jit(solution)/shard_map/pallas_call | solution.py:451

commit v3 on v2

v3 whole, which is shorter than its diff:
```python
import functools

import jax
import jax.numpy as jnp
from jax import lax
from jax.experimental import pallas as pl
from jax.experimental.pallas import tpu as pltpu
from jax.sharding import PartitionSpec as P

SPLIT = 4
MOST = 16
LOWRANK_SCALE = 2.0
LEVEL_STEP = 1.0 / 4096.0
F32 = jnp.float32
BF16 = jnp.bfloat16
FWD, BWD = 0, 1
LEFT, RIGHT = 0, 1


def dot_nt(a, b):
    return lax.dot_general(a, b, (((1,), (1,)), ((), ())), preferred_element_type=F32)


def dot_nn(a, b):
    return jnp.dot(a, b, preferred_element_type=F32)


def kernel(
    choice_hbm, steps_hbm, at_hbm, tok_hbm, cot_hbm, wg_hbm, wu_hbm, wd_hbm, bup_hbm,
    soon_v, back, mix_in, bg_v, ag_ref,
    rows_v, wg, wu, wd, bup, send, recv, pre_gate_v, pre_up_v, hid_v, lr_v,
    part, from_a, sum_b, from_b, fin, mix, lat, lat_in, bsend, routes, at_v,
    load_sem, sent_sem, y_sem, near_sem, rest_sem, a_sem, b_sem, c_sem, mix_sem, lat_sem, bg_sem,
):
    half = recv.shape[-1]
    units = wg.shape[0]
    tokens = rows_v.shape[1]
    n_section = lax.axis_size("section")
    s = lax.axis_index("section")
    me = lax.axis_index("expert")
    y, x = me // SPLIT, me % SPLIT
    xr, xo, xl = (x + 1) % SPLIT, (x + 2) % SPLIT, (x + 3) % SPLIT
    first, last = 1 - s % 2, s % 2

    def dev(row, col, sec=s):
        return {"section": sec, "expert": row * SPLIT + col}

    def toward(ph):
        return (s + n_section + 1 - 2 * ph) % n_section

    beside = (dev(y, xl), dev(y, xr))

    def copy(src, dst, kind, recv_sem, device):
        return pltpu.make_async_remote_copy(
            src_ref=src, dst_ref=dst, send_sem=sent_sem.at[kind], recv_sem=recv_sem,
            device_id=device, device_id_type=pl.DeviceIdType.MESH,
        )

    def wait(sem, ref):
        pltpu.make_async_copy(ref, ref, sem).wait()

    def loop(first, last, body):
        def step(k, _):
            body(k)
            return 0
        lax.fori_loop(first, last, step, 0)

    loads = [
        pltpu.make_async_copy(src, dst, load_sem.at[i])
        for i, src, dst in (
            (0, choice_hbm, routes.at[0]), (0, steps_hbm, routes.at[1]), (1, tok_hbm, rows_v.at[FWD]),
            (2, cot_hbm, rows_v.at[BWD]), (3, at_hbm, at_v), (4, wg_hbm, wg), (5, wu_hbm, wu),
            (6, wd_hbm, wd), (7, bup_hbm.at[y], bup),
        )
    ]
    for load in loads:
        load.start()

    barrier = pltpu.get_barrier_semaphore()
    partners = [dev(y, xl), dev(y, xr), dev(y, xo)]
    partners += [dev((y + k) % SPLIT, x) for k in range(1, SPLIT)]
    partners += [dev((y + k) % SPLIT, x, sec) for k in range(SPLIT) for sec in (toward(FWD), toward(BWD))]
    for device in partners:
        pl.semaphore_signal(barrier, inc=1, device_id=device, device_id_type=pl.DeviceIdType.MESH)

    shape = (SPLIT * MOST, tokens)
    row = lax.broadcasted_iota(jnp.int32, shape, 0)
    slot = row % MOST
    expert = (y + SPLIT - row // MOST) % SPLIT
    square = (tokens, tokens)
    earlier = lax.broadcasted_iota(jnp.int32, square, 0) < lax.broadcasted_iota(jnp.int32, square, 1)
    earlier = earlier.astype(F32).astype(BF16)
    wait(load_sem.at[0], routes)
    routed = jnp.zeros(shape, jnp.int32)
    gate = jnp.zeros(shape, jnp.int32)
    for j in range(routes.shape[1]):
        hit = routes[0, j:j + 1, :] == expert
        routed = jnp.where(hit, 1, routed)
        gate = jnp.where(hit, routes[1, j:j + 1, :], gate)
    taken = dot_nn(routed.astype(F32).astype(BF16), earlier)
    placed = (routed > 0) & (taken == slot.astype(F32))
    place = jnp.where(placed, 1.0, 0.0).astype(F32)
    weight = place * (gate.astype(F32) * LEVEL_STEP)
    slot_gate = jnp.sum(weight, axis=1, keepdims=True)
    place_half = place.astype(BF16)

    def dispatch(ph):
        for h in range(2):
            out = dot_nn(place_half, rows_v[ph, :, h * half:(h + 1) * half])
            if ph == BWD:
                out = out * slot_gate
            out = out.astype(BF16)
            recv[ph, 0, h, pl.ds(x, 1)] = out[:MOST][None]
            for k in range(1, SPLIT):
                send[ph, k, h] = out[k * MOST:(k + 1) * MOST]

    def y_start(ph, k):
        for h in range(2):
            copy(send.at[ph, k, h], recv.at[ph, k, h, x], ph, y_sem.at[ph, k],
                 dev((y + SPLIT - k) % SPLIT, x)).start()

    def x1_start(ph, k):
        for turn in range(2):
            for way in (LEFT, RIGHT):
                h = way if turn == 0 else 1 - way
                block = recv.at[ph, k, h, x]
                copy(block, block, 2, (near_sem, rest_sem)[turn].at[ph, k], beside[way]).start()

    def y_wait(ph, k):
        wait(y_sem.at[ph, k], send.at[ph, k])
        x1_start(ph, k)

    def x2_start(ph, k):
        wait(near_sem.at[ph, k], from_a.at[ph, k])
        for way in (LEFT, RIGHT):
            block = recv.at[ph, k, way, (xr, xl)[way]]
            copy(block, block, 3, rest_sem.at[ph, k], beside[way]).start()

    def gathered(ph, k):
        wait(rest_sem.at[ph, k], from_b.at[ph, k])

    def a_start(ph, k):
        for way in (LEFT, RIGHT):
            copy(part.at[ph, k, way, xo], from_a.at[ph, k, way], 4, a_sem.at[ph, k],
                 beside[way]).start()

    def b_start(ph, k):
        for way in (LEFT, RIGHT):
            copy(part.at[ph, k, 1 - way, (xl, xr)[way]], from_b.at[ph, k, way, 1 - way], 5,
                 b_sem.at[ph, k], beside[way]).start()

    def relay(ph, k):
        wait(a_sem.at[ph, k], from_a.at[ph, k])
        for way in (LEFT, RIGHT):
            mine = part[ph, k, way, pl.ds((xl, xr)[way], 1)][0].astype(F32)
            sum_b[ph, k, way] = (mine + from_a[ph, k, way].astype(F32)).astype(BF16)
            copy(sum_b.at[ph, k, way], from_b.at[ph, k, way, way], 5, b_sem.at[ph, k],
                 beside[way]).start()

    def finish(ph, k):
        wait(b_sem.at[ph, k], from_b.at[ph, k])
        for h in range(2):
            total = part[ph, k, h, pl.ds(x, 1)][0].astype(F32)
            total = total + from_b[ph, k, LEFT, h].astype(F32) + from_b[ph, k, RIGHT, h].astype(F32)
            fin[ph, k, h] = total.astype(BF16)
        copy(fin.at[ph, k], back.at[ph, k], 6, c_sem.at[ph],
             dev((y + k) % SPLIT, x, toward(ph))).start()

    def rows_of(ph, k, h):
        return recv[ph, k, h].reshape(SPLIT * MOST, half)

    def forward(k):
        pre_gate = dot_nt(rows_of(FWD, k, 0), wg[:, :half]) + dot_nt(rows_of(FWD, k, 1), wg[:, half:])
        pre_up = dot_nt(rows_of(FWD, k, 0), wu[:, :half]) + dot_nt(rows_of(FWD, k, 1), wu[:, half:])
        hidden = (pre_gate * jax.nn.sigmoid(pre_gate) * pre_up).astype(BF16)
        pre_gate_v[k] = pre_gate
        pre_up_v[k] = pre_up
        hid_v[k] = hidden
        latent = dot_nt(hidden, at_v[...]).astype(BF16)
        latent = (LOWRANK_SCALE * latent.astype(F32)).astype(BF16)
        for h in range(2):
            cols = slice(h * half, (h + 1) * half)
            out = dot_nn(hidden, wd[:, cols]) + dot_nn(latent, bup[:, cols])
            part[FWD, k, h] = out.astype(BF16).reshape(SPLIT, MOST, half)

    def backward(k):
        low = dot_nt(rows_of(BWD, k, 0), bup[:, :half]) + dot_nt(rows_of(BWD, k, 1), bup[:, half:])
        low = (LOWRANK_SCALE * low).astype(BF16)
        lr_v[k] = low
        grad_hidden = dot_nt(rows_of(BWD, k, 0), wd[:, :half]) + dot_nt(rows_of(BWD, k, 1), wd[:, half:])
        grad_hidden = grad_hidden + dot_nn(low, at_v[...])
        pre_gate, pre_up = pre_gate_v[k], pre_up_v[k]
        sig = jax.nn.sigmoid(pre_gate)
        grad_gate = (grad_hidden * pre_up * sig * (1.0 + pre_gate * (1.0 - sig))).astype(BF16)
        grad_up = (grad_hidden * pre_gate * sig).astype(BF16)
        for h in range(2):
            cols = slice(h * half, (h + 1) * half)
            out = dot_nn(grad_gate, wg[:, cols]) + dot_nn(grad_up, wu[:, cols])
            part[BWD, k, h] = out.astype(BF16).reshape(SPLIT, MOST, half)

    loads[2].wait()
    dispatch(FWD)
    pl.semaphore_wait(barrier, len(partners))
    x1_start(FWD, 0)
    y_start(FWD, 1)
    y_start(FWD, 3)

    loads[3].wait()
    dispatch(BWD)
    x1_start(BWD, 0)
    y_start(BWD, 1)
    y_start(BWD, 3)
    y_start(FWD, 2)
    y_start(BWD, 2)

    high = weight.astype(BF16).astype(F32)
    mixes = (jnp.concatenate([high, weight - high], axis=0),
             jnp.concatenate([place, jnp.zeros_like(place)], axis=0))
    for ph in (FWD, BWD):
        mix[ph] = jnp.transpose(mixes[ph]).astype(BF16)
        copy(mix.at[ph], mix_in.at[ph], 7, mix_sem.at[ph], dev(y, x, toward(ph))).start()

    def both(step, k):
        step(FWD, k)
        step(BWD, k)

    both(y_wait, 1)
    both(x2_start, 0)
    both(y_wait, 3)
    both(x2_start, 1)
    both(y_wait, 2)
    for load in loads[4:]:
        load.wait()

    def chunk(i):
        return i + i // 2 - 2 * (i // 3)

    def compute_step(i):
        k = chunk(i)
        both(gathered, k)
        forward(k)
        backward(k)
        a_start(first, k)
        b_start(first, k)
        pl.when(i < 2)(lambda: both(x2_start, chunk(i + 2)))
        pl.when(i == 1)(ahead)
        pl.when(i == 2)(lambda: relay(first, 1))

    def ahead():
        relay(first, 0)
        a_start(last, 1)
        b_start(last, 1)

    loop(0, SPLIT, compute_step)
    relay(first, 3)
    a_start(last, 2)
    relay(last, 1)

    hidden_all = hid_v[...].reshape(SPLIT * SPLIT * MOST, units)
    lat[...] = dot_nt(at_v[...], hidden_all).astype(BF16)
    for i, device in enumerate(beside + (dev(y, xo),)):
        copy(lat, lat_in.at[i], 8, lat_sem, device).start()

    relay(first, 2)
    a_start(last, 3)
    b_start(last, 2)
    for k in (0, 1, 3):
        finish(first, k)
    relay(last, 2)
    a_start(last, 0)
    b_start(last, 3)

    ag_ref[...] = lax.dot_general(
        lr_v[...].reshape(SPLIT * SPLIT * MOST, lr_v.shape[-1]),
        hid_v[...].reshape(SPLIT * SPLIT * MOST, units),
        (((0,), (0,)), ((), ())), preferred_element_type=F32)

    width = bg_v.shape[-1]
    wait(lat_sem, lat_in)
    lat_sum = lat[...].astype(F32)
    for i in range(3):
        lat_sum = lat_sum + lat_in[i].astype(F32)
    lat_sum = LOWRANK_SCALE * lat_sum
    lat_high = lat_sum.astype(BF16)
    lat_low = (lat_sum - lat_high.astype(F32)).astype(BF16)

    per_half = half // width
    for k in range(SPLIT):
        block = ((y + k) % SPLIT) * SPLIT + x
        cols = pl.ds(pl.multiple_of((block % per_half) * width, width), width)
        grad_rows = recv[BWD, :, pl.ds(block // per_half, 1), :, :, cols]
        grad_rows = grad_rows.reshape(SPLIT * SPLIT * MOST, width)
        value = dot_nn(lat_high, grad_rows) + dot_nn(lat_low, grad_rows)
        if k == 0:
            bg_v[pl.ds(y, 1)] = value[None]
        else:
            bsend[k] = value
            copy(bsend.at[k], bg_v.at[y], 9, bg_sem, dev((y + k) % SPLIT, x)).start()

    finish(last, 1)
    finish(first, 2)
    relay(last, 3)
    b_start(last, 0)
    finish(last, 2)
    relay(last, 0)
    finish(last, 3)
    finish(last, 0)

    def arrived(ph):
        wait(mix_sem.at[ph], mix_in.at[ph])
        wait(c_sem.at[ph], back.at[ph])

    soon, late = last, first
    arrived(soon)
    for cols, value in spread(mix_in.at[soon], back.at[soon]):
        soon_v[:, cols] = value
    wait(bg_sem, bsend.at[pl.ds(1, SPLIT - 1)])
    for kind, ref in (
        (FWD, send.at[FWD, pl.ds(1, SPLIT - 1)]), (BWD, send.at[BWD, pl.ds(1, SPLIT - 1)]),
        (2, recv.at[FWD]), (3, send), (4, send), (5, recv.at[FWD]), (6, send), (7, mix), (8, lat_in),
        (9, bsend.at[pl.ds(1, SPLIT - 1)]),
    ):
        wait(sent_sem.at[kind], ref)
    arrived(late)


def spread(mix, rows):
    half = rows.shape[-1]
    tile = min(512, half)
    for h in range(2):
        for n in range(0, half, tile):
            block = rows[:, h, :, n:n + tile].reshape(SPLIT * MOST, tile)
            block = jnp.concatenate([block, block], axis=0)
            yield slice(h * half + n, h * half + n + tile), dot_nn(mix[...], block).astype(BF16)


def last_kernel(
    soon_v, back, mix_in, bg_v, ag_v, out_hbm, grad_hbm, bg_hbm, ag_hbm, late_v, sem, late_sem
):
    even = lax.axis_index("section") % 2 == 0
    small = [pltpu.make_async_copy(bg_v, bg_hbm, sem.at[1]), pltpu.make_async_copy(ag_v, ag_hbm, sem.at[2])]

    def write(late, soon_hbm, late_hbm):
        copies = [pltpu.make_async_copy(soon_v, soon_hbm, sem.at[0])]
        copies[0].start()
        for i, (cols, value) in enumerate(spread(mix_in.at[late], back.at[late])):
            late_v[:, cols] = value
            copies.append(
                pltpu.make_async_copy(late_v.at[:, cols], late_hbm.at[:, cols], late_sem.at[i]))
            copies[-1].start()
        for copy in copies:
            copy.wait()

    for copy in small:
        copy.start()
    pl.when(even)(lambda: write(BWD, out_hbm, grad_hbm))
    pl.when(jnp.logical_not(even))(lambda: write(FWD, grad_hbm, out_hbm))
    for copy in small:
        copy.wait()


def on_device(
    section_layer_input, token_expert_choice, route_gate_steps, gate_weight, up_weight, down_weight,
    adapter_down_maps, adapter_up_maps, cotangent,
):
    tokens, width = section_layer_input.shape[1:]
    units = gate_weight.shape[1]
    rank = adapter_down_maps.shape[2]
    half = width // 2
    cols = width // lax.axis_size("expert")
    dma = pltpu.SemaphoreType.DMA
    flight = SPLIT * MOST
    tiles = width // min(512, half)
    hbm = pl.BlockSpec(memory_space=pltpu.HBM)
    vmem = pl.BlockSpec(memory_space=pltpu.VMEM)
    held = pl.pallas_call(
        kernel,
        out_shape=(
            jax.ShapeDtypeStruct((tokens, width), BF16),
            jax.ShapeDtypeStruct((2, SPLIT, 2, MOST, half), BF16),
            jax.ShapeDtypeStruct((2, tokens, 2 * flight), BF16),
            jax.ShapeDtypeStruct((SPLIT, rank, cols), F32),
            jax.ShapeDtypeStruct((rank, units), F32),
        ),
        in_specs=[hbm] * 9,
        out_specs=(vmem,) * 5,
        scratch_shapes=[
            pltpu.VMEM((2, tokens, width), BF16),
            pltpu.VMEM((units, width), BF16),
            pltpu.VMEM((units, width), BF16),
            pltpu.VMEM((units, width), BF16),
            pltpu.VMEM((rank, width), BF16),
            pltpu.VMEM((2, SPLIT, 2, MOST, half), BF16),
            pltpu.VMEM((2, SPLIT, 2, SPLIT, MOST, half), BF16),
            pltpu.VMEM((SPLIT, flight, units), F32),
            pltpu.VMEM((SPLIT, flight, units), F32),
            pltpu.VMEM((SPLIT, flight, units), BF16),
            pltpu.VMEM((SPLIT, flight, rank), BF16),
            pltpu.VMEM((2, SPLIT, 2, SPLIT, MOST, half), BF16),
            pltpu.VMEM((2, SPLIT, 2, MOST, half), BF16),
            pltpu.VMEM((2, SPLIT, 2, MOST, half), BF16),
            pltpu.VMEM((2, SPLIT, 2, 2, MOST, half), BF16),
            pltpu.VMEM((2, SPLIT, 2, MOST, half), BF16),
            pltpu.VMEM((2, tokens, 2 * flight), BF16),
            pltpu.VMEM((rank, SPLIT * flight), BF16),
            pltpu.VMEM((3, rank, SPLIT * flight), BF16),
            pltpu.VMEM((SPLIT, rank, cols), F32),
            pltpu.VMEM((2,) + token_expert_choice.shape[:0:-1], jnp.int32),
            pltpu.VMEM((rank, units), BF16),
            dma((8,)),
            dma((10,)),
            dma((2, SPLIT)),
            dma((2, SPLIT)),
            dma((2, SPLIT)),
            dma((2, SPLIT)),
            dma((2, SPLIT)),
            dma((2,)),
            dma((2,)),
            dma, dma,
        ],
        compiler_params=pltpu.CompilerParams(
            collective_id=0, has_side_effects=True, vmem_limit_bytes=48 * 1024 * 1024),
    )(
        *[pltpu.with_memory_space_constraint(a, pltpu.HBM) for a in (token_expert_choice[0].T, route_gate_steps[0].T, adapter_down_maps[0].T,
        section_layer_input[0], cotangent[0], gate_weight[0], up_weight[0], down_weight[0],
        adapter_up_maps[0])],
    )
    out, grad, b_grad, a_grad = pl.pallas_call(
        last_kernel,
        out_shape=(
            jax.ShapeDtypeStruct((tokens, width), BF16),
            jax.ShapeDtypeStruct((tokens, width), BF16),
            jax.ShapeDtypeStruct((SPLIT, rank, cols), F32),
            jax.ShapeDtypeStruct((rank, units), F32),
        ),
        in_specs=[vmem] * 5,
        out_specs=(hbm,) * 4,
        scratch_shapes=[pltpu.VMEM((tokens, width), BF16), dma((3,)), dma((tiles,))],
        compiler_params=pltpu.CompilerParams(vmem_limit_bytes=16 * 1024 * 1024),
    )(*held)
    return out[None], grad[None], a_grad.T[None], b_grad[None]


def solution(mesh):
    tokens = P("section", "expert", None)
    return jax.shard_map(
        on_device,
        mesh=mesh,
        in_specs=(tokens,) * 7 + (P("section", None, None, None), tokens),
        out_specs=(tokens, tokens, tokens, P("section", None, None, "expert")),
        check_vma=False,
    )
```

time: 89.8 us -> 82.3 us (0.916); the launches traced: 88.7 us -> 82.2 us
  Pallas kernels: 88.1 us -> 81.6 us
    pallas_call x1, Pallas kernels: 86.7 us -> 80 us  [on_device(): pl.pallas_call(kernel, out_shape=(jax.ShapeDtypeStruct((tokens, width), B...]
where the time goes in v3:
time: 82.3 us; the launch traced here: 82.2 us
  Pallas kernels  81.6 us (99%)
    pallas_call x1, Pallas kernels, on_device(): pl.pallas_call(kernel, out_shape=(jax.ShapeDtypeStruct((tokens, width), B...  80 us

profile of v3, /device:TPU:1, one launch (start us, length us, event | category | flops | bytes accessed | tf_op | source)
XLA Modules:
  0.0 82.2 jit_solution(13708464572401079330)
XLA Ops:
  0.6 80.0 %shard_map.120 = (bf16[128,4096]{1,0:T(8,128)(2,1)S(1)}, bf16[2,4,2,16,2048]{4,3,2,1,0:T(8,128)(2,1)S(1)}, bf16[2,128,128]{2,1,0:T(8,128)(2,1)S(1)}, f32[4,16,256]{2,1,0:T(8,128)S(1)}, f32[16,256]{1,0:T(8,128)S(1)}) custom-call(s32[8,128]{1,0:T(8,128)} %bitcast.28, s32[8,128]{1,0:T(8,128)} %bitcast.29, bf16[16,256]{1,0:T(8,128)(2,1)} %bitcast.27, ...), custom_call_target="tpu_custom_call" | custom-call | tf_op jit(solution)/shard_map/pallas_call | solution.py:376
  80.6 1.6 %shard_map.121 = (bf16[128,4096]{1,0:T(8,128)(2,1)}, bf16[128,4096]{1,0:T(8,128)(2,1)}, f32[4,16,256]{2,1,0:T(8,128)}, f32[16,256]{1,0:T(8,128)}) custom-call(bf16[128,4096]{1,0:T(8,128)(2,1)S(1)} %get-tuple-element.13.soon_v, bf16[2,4,2,16,2048]{4,3,2,1,0:T(8,128)(2,1)S(1)} %get-tuple-element.14.back, bf16[2,128,128]{2,1,0:T(8,128)(2,1)S(1)} %get-tuple-element.15.mix_in, ...), custom_call_target="tpu_custom_call" | custom-call | tf_op jit(solution)/shard_map/pallas_call | solution.py:428

commit v4 on v3

--- a/solution.py
+++ b/solution.py
@@ -30,7 +30,7 @@
     soon_v, back, mix_in, bg_v, ag_ref,
     rows_v, wg, wu, wd, bup, send, recv, pre_gate_v, pre_up_v, hid_v, lr_v,
     part, from_a, sum_b, from_b, fin, mix, lat, lat_in, bsend, routes, at_v,
-    load_sem, sent_sem, y_sem, near_sem, rest_sem, a_sem, b_sem, c_sem, mix_sem, lat_sem, bg_sem,
+    load_sem, sent_sem, y_sem, near_sem, rest_sem, a_sem, b_sem, c_sem, mix_sem, lat_sem, bg_sem, ready, go,
 ):
     half = recv.shape[-1]
     units = wg.shape[0]
@@ -65,23 +65,58 @@
             return 0
         lax.fori_loop(first, last, step, 0)
 
-    loads = [
-        pltpu.make_async_copy(src, dst, load_sem.at[i])
-        for i, src, dst in (
-            (0, choice_hbm, routes.at[0]), (0, steps_hbm, routes.at[1]), (1, tok_hbm, rows_v.at[FWD]),
-            (2, cot_hbm, rows_v.at[BWD]), (3, at_hbm, at_v), (4, wg_hbm, wg), (5, wu_hbm, wu),
-            (6, wd_hbm, wd), (7, bup_hbm.at[y], bup),
-        )
-    ]
-    for load in loads:
-        load.start()
-
+    def load(i, src, dst, pieces=1):
+        rows = src.shape[0] // pieces
+        for piece in range(pieces):
+            at = pl.ds(piece * rows, rows)
+            pltpu.make_async_copy(src.at[at], dst.at[at], load_sem.at[i]).start()
+
+    load(0, choice_hbm, routes.at[0])
+    load(0, steps_hbm, routes.at[1])
+    load(1, tok_hbm, rows_v.at[FWD], 4)
+
+    def gate_of(sec):
+        return SPLIT * SPLIT - 1 - (SPLIT + 1) * (1 - sec % 2)
+
+    def signal(sem, device):
+        pl.semaphore_signal(sem, inc=1, device_id=device, device_id_type=pl.DeviceIdType.MESH)
+
+    n_expert = SPLIT * SPLIT
+    gate_me = gate_of(s)
+    at_gate = me == gate_me
+    elsewhere = jnp.logical_not(at_gate)
     barrier = pltpu.get_barrier_semaphore()
-    partners = [dev(y, xl), dev(y, xr), dev(y, xo)]
-    partners += [dev((y + k) % SPLIT, x) for k in range(1, SPLIT)]
-    partners += [dev((y + k) % SPLIT, x, sec) for k in range(SPLIT) for sec in (toward(FWD), toward(BWD))]
-    for device in partners:
-        pl.semaphore_signal(barrier, inc=1, device_id=device, device_id_type=pl.DeviceIdType.MESH)
+
+    def tell_all(sem):
+        def step(j):
+            signal(sem, {"section": s, "expert": (me + j) % n_expert})
+        loop(1, n_expert, step)
+
+    def tell_partners():
+        partners = [(y, xl), (y, xr), (y, xo)] + [((y + k) % SPLIT, x) for k in range(1, SPLIT)]
+        for row, col in partners:
+            pl.when(row * SPLIT + col != gate_me)(functools.partial(signal, barrier, dev(row, col)))
+
+    def enter():
+        beside_gate = jnp.logical_or(y == gate_me // SPLIT, x == gate_me % SPLIT)
+        pl.semaphore_wait(barrier, jnp.where(beside_gate, 2 * SPLIT - 2, 2 * SPLIT - 1))
+        signal(ready, {"section": s, "expert": gate_me})
+
+    def enter_gate():
+        pl.semaphore_wait(ready, n_expert - 1)
+        for ph in (FWD, BWD):
+            signal(barrier, {"section": toward(ph), "expert": gate_of(toward(ph))})
+
+    def pass_on():
+        pl.semaphore_wait(barrier, 2)
+        tell_all(go)
+
+    pl.when(at_gate)(lambda: tell_all(barrier))
+    pl.when(elsewhere)(tell_partners)
+    load(2, cot_hbm, rows_v.at[BWD], 4)
+    weights = ((at_hbm, at_v), (wg_hbm, wg), (wu_hbm, wu), (wd_hbm, wd), (bup_hbm.at[y], bup))
+    for i, (src, dst) in enumerate(weights):
+        load(3 + i, src, dst)
 
     shape = (SPLIT * MOST, tokens)
     row = lax.broadcasted_iota(jnp.int32, shape, 0)
@@ -198,14 +233,15 @@
             out = dot_nn(grad_gate, wg[:, cols]) + dot_nn(grad_up, wu[:, cols])
             part[BWD, k, h] = out.astype(BF16).reshape(SPLIT, MOST, half)
 
-    loads[2].wait()
+    wait(load_sem.at[1], rows_v.at[FWD])
     dispatch(FWD)
-    pl.semaphore_wait(barrier, len(partners))
+    pl.when(elsewhere)(enter)
+    pl.when(at_gate)(enter_gate)
     x1_start(FWD, 0)
     y_start(FWD, 1)
     y_start(FWD, 3)
 
-    loads[3].wait()
+    wait(load_sem.at[2], rows_v.at[BWD])
     dispatch(BWD)
     x1_start(BWD, 0)
     y_start(BWD, 1)
@@ -218,7 +254,6 @@
              jnp.concatenate([place, jnp.zeros_like(place)], axis=0))
     for ph in (FWD, BWD):
         mix[ph] = jnp.transpose(mixes[ph]).astype(BF16)
-        copy(mix.at[ph], mix_in.at[ph], 7, mix_sem.at[ph], dev(y, x, toward(ph))).start()
 
     def both(step, k):
         step(FWD, k)
@@ -229,8 +264,8 @@
     both(y_wait, 3)
     both(x2_start, 1)
     both(y_wait, 2)
-    for load in loads[4:]:
-        load.wait()
+    for i, (_, dst) in enumerate(weights):
+        wait(load_sem.at[3 + i], dst)
 
     def chunk(i):
         return i + i // 2 - 2 * (i // 3)
@@ -251,6 +286,7 @@
         a_start(last, 1)
         b_start(last, 1)
 
+    pl.when(at_gate)(pass_on)
     loop(0, SPLIT, compute_step)
     relay(first, 3)
     a_start(last, 2)
@@ -264,6 +300,9 @@
     relay(first, 2)
     a_start(last, 3)
     b_start(last, 2)
+    pl.when(elsewhere)(lambda: pl.semaphore_wait(go, 1))
+    for ph in (FWD, BWD):
+        copy(mix.at[ph], mix_in.at[ph], 7, mix_sem.at[ph], dev(y, x, toward(ph))).start()
     for k in (0, 1, 3):
         finish(first, k)
     relay(last, 2)
@@ -304,7 +343,6 @@
     finish(last, 2)
     relay(last, 0)
     finish(last, 3)
-    finish(last, 0)
 
     def arrived(ph):
         wait(mix_sem.at[ph], mix_in.at[ph])
@@ -314,6 +352,7 @@
     arrived(soon)
     for cols, value in spread(mix_in.at[soon], back.at[soon]):
         soon_v[:, cols] = value
+    finish(last, 0)
     wait(bg_sem, bsend.at[pl.ds(1, SPLIT - 1)])
     for kind, ref in (
         (FWD, send.at[FWD, pl.ds(1, SPLIT - 1)]), (BWD, send.at[BWD, pl.ds(1, SPLIT - 1)]),
@@ -341,8 +380,11 @@
     small = [pltpu.make_async_copy(bg_v, bg_hbm, sem.at[1]), pltpu.make_async_copy(ag_v, ag_hbm, sem.at[2])]
 
     def write(late, soon_hbm, late_hbm):
-        copies = [pltpu.make_async_copy(soon_v, soon_hbm, sem.at[0])]
-        copies[0].start()
+        copies = []
+        rows = soon_v.shape[0] // 8
+        for i in range(8):
+            at = pl.ds(i * rows, rows)
+            pltpu.make_async_copy(soon_v.at[at], soon_hbm.at[at], sem.at[0]).start()
         for i, (cols, value) in enumerate(spread(mix_in.at[late], back.at[late])):
             late_v[:, cols] = value
             copies.append(
@@ -350,6 +392,7 @@
             copies[-1].start()
         for copy in copies:
             copy.wait()
+        pltpu.make_async_copy(soon_v, soon_hbm, sem.at[0]).wait()
 
     for copy in small:
         copy.start()
@@ -417,6 +460,7 @@
             dma((2,)),
             dma((2,)),
             dma, dma,
+            pltpu.SemaphoreType.REGULAR, pltpu.SemaphoreType.REGULAR,
         ],
         compiler_params=pltpu.CompilerParams(
             collective_id=0, has_side_effects=True, vmem_limit_bytes=48 * 1024 * 1024),

time: 82.3 us -> 80.8 us (0.982)
  Pallas kernels: 81.6 us -> 80 us
    pallas_call x1, Pallas kernels: 80 us -> 78.4 us  [on_device(): pl.pallas_call(kernel, out_shape=(jax.ShapeDtypeStruct((tokens, width), B...]
where the time goes in v4:
time: 80.8 us; the launch traced here: 80.7 us
  Pallas kernels  80 us (99%)
    pallas_call x1, Pallas kernels, on_device(): pl.pallas_call(kernel, out_shape=(jax.ShapeDtypeStruct((tokens, width), B...  78.4 us

profile of v4, /device:TPU:1, one launch (start us, length us, event | category | flops | bytes accessed | tf_op | source)
XLA Modules:
  0.0 80.7 jit_solution(1769385471172493908)
XLA Ops:
  0.6 78.4 %shard_map.120 = (bf16[128,4096]{1,0:T(8,128)(2,1)S(1)}, bf16[2,4,2,16,2048]{4,3,2,1,0:T(8,128)(2,1)S(1)}, bf16[2,128,128]{2,1,0:T(8,128)(2,1)S(1)}, f32[4,16,256]{2,1,0:T(8,128)S(1)}, f32[16,256]{1,0:T(8,128)S(1)}) custom-call(s32[8,128]{1,0:T(8,128)} %bitcast.28, s32[8,128]{1,0:T(8,128)} %bitcast.29, bf16[16,256]{1,0:T(8,128)(2,1)} %bitcast.27, ...), custom_call_target="tpu_custom_call" | custom-call | tf_op jit(solution)/shard_map/pallas_call | solution.py:419
  79.1 1.6 %shard_map.121 = (bf16[128,4096]{1,0:T(8,128)(2,1)}, bf16[128,4096]{1,0:T(8,128)(2,1)}, f32[4,16,256]{2,1,0:T(8,128)}, f32[16,256]{1,0:T(8,128)}) custom-call(bf16[128,4096]{1,0:T(8,128)(2,1)S(1)} %get-tuple-element.13.soon_v, bf16[2,4,2,16,2048]{4,3,2,1,0:T(8,128)(2,1)S(1)} %get-tuple-element.14.back, bf16[2,128,128]{2,1,0:T(8,128)(2,1)S(1)} %get-tuple-element.15.mix_in, ...), custom_call_target="tpu_custom_call" | custom-call | tf_op jit(solution)/shard_map/pallas_call | solution.py:472

commit v5 on v4

--- a/solution.py
+++ b/solution.py
@@ -159,7 +159,7 @@
             for way in (LEFT, RIGHT):
                 h = way if turn == 0 else 1 - way
                 block = recv.at[ph, k, h, x]
-                copy(block, block, 2, (near_sem, rest_sem)[turn].at[ph, k], beside[way]).start()
+                copy(block, block, 2, (near_sem.at[ph, k], rest_sem.at[k])[turn], beside[way]).start()
 
     def y_wait(ph, k):
         wait(y_sem.at[ph, k], send.at[ph, k])
@@ -169,10 +169,10 @@
         wait(near_sem.at[ph, k], from_a.at[ph, k])
         for way in (LEFT, RIGHT):
             block = recv.at[ph, k, way, (xr, xl)[way]]
-            copy(block, block, 3, rest_sem.at[ph, k], beside[way]).start()
-
-    def gathered(ph, k):
-        wait(rest_sem.at[ph, k], from_b.at[ph, k])
+            copy(block, block, 3, rest_sem.at[k], beside[way]).start()
+
+    def gathered(k):
+        wait(rest_sem.at[k], from_b.at[:, k])
 
     def a_start(ph, k):
         for way in (LEFT, RIGHT):
@@ -198,8 +198,8 @@
             total = part[ph, k, h, pl.ds(x, 1)][0].astype(F32)
             total = total + from_b[ph, k, LEFT, h].astype(F32) + from_b[ph, k, RIGHT, h].astype(F32)
             fin[ph, k, h] = total.astype(BF16)
-        copy(fin.at[ph, k], back.at[ph, k], 6, c_sem.at[ph],
-             dev((y + k) % SPLIT, x, toward(ph))).start()
+            copy(fin.at[ph, k, h], back.at[ph, k, h], 6, c_sem.at[ph],
+                 dev((y + k) % SPLIT, x, toward(ph))).start()
 
     def rows_of(ph, k, h):
         return recv[ph, k, h].reshape(SPLIT * MOST, half)
@@ -244,10 +244,6 @@
     wait(load_sem.at[2], rows_v.at[BWD])
     dispatch(BWD)
     x1_start(BWD, 0)
-    y_start(BWD, 1)
-    y_start(BWD, 3)
-    y_start(FWD, 2)
-    y_start(BWD, 2)
 
     high = weight.astype(BF16).astype(F32)
     mixes = (jnp.concatenate([high, weight - high], axis=0),
@@ -259,9 +255,16 @@
         step(FWD, k)
         step(BWD, k)
 
-    both(y_wait, 1)
-    both(x2_start, 0)
-    both(y_wait, 3)
+    y_wait(FWD, 1)
+    y_start(BWD, 1)
+    y_start(BWD, 3)
+    x2_start(FWD, 0)
+    y_wait(FWD, 3)
+    y_start(FWD, 2)
+    y_wait(BWD, 1)
+    y_start(BWD, 2)
+    x2_start(BWD, 0)
+    y_wait(BWD, 3)
     both(x2_start, 1)
     both(y_wait, 2)
     for i, (_, dst) in enumerate(weights):
@@ -272,7 +275,7 @@
 
     def compute_step(i):
         k = chunk(i)
-        both(gathered, k)
+        gathered(k)
         forward(k)
         backward(k)
         a_start(first, k)
@@ -454,7 +457,7 @@
             dma((10,)),
             dma((2, SPLIT)),
             dma((2, SPLIT)),
-            dma((2, SPLIT)),
+            dma((SPLIT,)),
             dma((2, SPLIT)),
             dma((2, SPLIT)),
             dma((2,)),

time: 80.8 us -> 80.3 us (level)
  no operation moved by 1% of the time
where the time goes in v5:
time: 80.3 us; the launch traced here: 80.2 us
  Pallas kernels  79.6 us (99%)
    pallas_call x1, Pallas kernels, on_device(): pl.pallas_call(kernel, out_shape=(jax.ShapeDtypeStruct((tokens, width), B...  78 us

profile of v5, /device:TPU:1, one launch (start us, length us, event | category | flops | bytes accessed | tf_op | source)
XLA Modules:
  0.0 80.2 jit_solution(9359498888605065994)
XLA Ops:
  0.6 78.0 %shard_map.120 = (bf16[128,4096]{1,0:T(8,128)(2,1)S(1)}, bf16[2,4,2,16,2048]{4,3,2,1,0:T(8,128)(2,1)S(1)}, bf16[2,128,128]{2,1,0:T(8,128)(2,1)S(1)}, f32[4,16,256]{2,1,0:T(8,128)S(1)}, f32[16,256]{1,0:T(8,128)S(1)}) custom-call(s32[8,128]{1,0:T(8,128)} %bitcast.28, s32[8,128]{1,0:T(8,128)} %bitcast.29, bf16[16,256]{1,0:T(8,128)(2,1)} %bitcast.27, ...), custom_call_target="tpu_custom_call" | custom-call | tf_op jit(solution)/shard_map/pallas_call | solution.py:422
  78.6 1.6 %shard_map.121 = (bf16[128,4096]{1,0:T(8,128)(2,1)}, bf16[128,4096]{1,0:T(8,128)(2,1)}, f32[4,16,256]{2,1,0:T(8,128)}, f32[16,256]{1,0:T(8,128)}) custom-call(bf16[128,4096]{1,0:T(8,128)(2,1)S(1)} %get-tuple-element.13.soon_v, bf16[2,4,2,16,2048]{4,3,2,1,0:T(8,128)(2,1)S(1)} %get-tuple-element.14.back, bf16[2,128,128]{2,1,0:T(8,128)(2,1)S(1)} %get-tuple-element.15.mix_in, ...), custom_call_target="tpu_custom_call" | custom-call | tf_op jit(solution)/shard_map/pallas_call | solution.py:475

commit v6 on v5

--- a/solution.py
+++ b/solution.py
@@ -51,6 +51,7 @@
     beside = (dev(y, xl), dev(y, xr))
 
     def copy(src, dst, kind, recv_sem, device):
+        kind = (0, 0, 1, 1, 1, 2, 3, 4, 5, 6)[kind]
         return pltpu.make_async_remote_copy(
             src_ref=src, dst_ref=dst, send_sem=sent_sem.at[kind], recv_sem=recv_sem,
             device_id=device, device_id_type=pl.DeviceIdType.MESH,
@@ -151,7 +152,7 @@
 
     def y_start(ph, k):
         for h in range(2):
-            copy(send.at[ph, k, h], recv.at[ph, k, h, x], ph, y_sem.at[ph, k],
+            copy(send.at[ph, k, h], recv.at[ph, k, h, x], ph, y_sem.at[ph, k - 1],
                  dev((y + SPLIT - k) % SPLIT, x)).start()
 
     def x1_start(ph, k):
@@ -162,7 +163,7 @@
                 copy(block, block, 2, (near_sem.at[ph, k], rest_sem.at[k])[turn], beside[way]).start()
 
     def y_wait(ph, k):
-        wait(y_sem.at[ph, k], send.at[ph, k])
+        wait(y_sem.at[ph, k - 1], send.at[ph, k])
         x1_start(ph, k)
 
     def x2_start(ph, k):
@@ -358,9 +359,8 @@
     finish(last, 0)
     wait(bg_sem, bsend.at[pl.ds(1, SPLIT - 1)])
     for kind, ref in (
-        (FWD, send.at[FWD, pl.ds(1, SPLIT - 1)]), (BWD, send.at[BWD, pl.ds(1, SPLIT - 1)]),
-        (2, recv.at[FWD]), (3, send), (4, send), (5, recv.at[FWD]), (6, send), (7, mix), (8, lat_in),
-        (9, bsend.at[pl.ds(1, SPLIT - 1)]),
+        (0, send.at[:, pl.ds(1, SPLIT - 1)]), (1, recv), (2, recv.at[FWD]), (3, send), (4, mix),
+        (5, lat_in), (6, bsend.at[pl.ds(1, SPLIT - 1)]),
     ):
         wait(sent_sem.at[kind], ref)
     arrived(late)
@@ -454,8 +454,8 @@
             pltpu.VMEM((2,) + token_expert_choice.shape[:0:-1], jnp.int32),
             pltpu.VMEM((rank, units), BF16),
             dma((8,)),
-            dma((10,)),
-            dma((2, SPLIT)),
+            dma((7,)),
+            dma((2, SPLIT - 1)),
             dma((2, SPLIT)),
             dma((SPLIT,)),
             dma((2, SPLIT)),

time: 80.3 us -> 80.3 us (level)
  no operation moved by 1% of the time
where the time goes in v6:
time: 80.3 us; the launch traced here: 80.2 us
  Pallas kernels  79.5 us (99%)
    pallas_call x1, Pallas kernels, on_device(): pl.pallas_call(kernel, out_shape=(jax.ShapeDtypeStruct((tokens, width), B...  77.9 us

profile of v6, /device:TPU:1, one launch (start us, length us, event | category | flops | bytes accessed | tf_op | source)
XLA Modules:
  0.0 80.2 jit_solution(17862777226482821165)
XLA Ops:
  0.6 77.9 %shard_map.120 = (bf16[128,4096]{1,0:T(8,128)(2,1)S(1)}, bf16[2,4,2,16,2048]{4,3,2,1,0:T(8,128)(2,1)S(1)}, bf16[2,128,128]{2,1,0:T(8,128)(2,1)S(1)}, f32[4,16,256]{2,1,0:T(8,128)S(1)}, f32[16,256]{1,0:T(8,128)S(1)}) custom-call(s32[8,128]{1,0:T(8,128)} %bitcast.28, s32[8,128]{1,0:T(8,128)} %bitcast.29, bf16[16,256]{1,0:T(8,128)(2,1)} %bitcast.27, ...), custom_call_target="tpu_custom_call" | custom-call | tf_op jit(solution)/shard_map/pallas_call | solution.py:422
  78.6 1.6 %shard_map.121 = (bf16[128,4096]{1,0:T(8,128)(2,1)}, bf16[128,4096]{1,0:T(8,128)(2,1)}, f32[4,16,256]{2,1,0:T(8,128)}, f32[16,256]{1,0:T(8,128)}) custom-call(bf16[128,4096]{1,0:T(8,128)(2,1)S(1)} %get-tuple-element.13.soon_v, bf16[2,4,2,16,2048]{4,3,2,1,0:T(8,128)(2,1)S(1)} %get-tuple-element.14.back, bf16[2,128,128]{2,1,0:T(8,128)(2,1)S(1)} %get-tuple-element.15.mix_in, ...), custom_call_target="tpu_custom_call" | custom-call | tf_op jit(solution)/shard_map/pallas_call | solution.py:475
